TPU v7x, 128 devices: a whole 4x4x4 slice. The times are simulated.
128 devices in a mesh: dp: 4 (over y), expert: 32 (over x, z, core).
Axes of the slice: x: 4, y: 4, z: 4, core: 2. Of those that a mesh axis runs over, the one named last changes fastest.
Arguments:
- tokens: bfloat16 [4096, 2048], P('expert', 'dp'), may hold values from -6 to 6
- picks: int32 [2, 4096, 16], P(None, 'expert'), may hold values from 0 to 255, all different within a row; in each aligned block of 128 rows (0 to 127, 128 to 255, ..., all dimensions but the last counted through in order) at most 10 rows name the same one
- halting: int32 [4096], P('expert'), may hold values from 1 to 2
- w_sel: bfloat16 [2048, 256], P('dp'), may hold values from -0.125 to 0.125
- w_up: bfloat16 [256, 2048, 256], P('expert', 'dp'), may hold values from -0.125 to 0.125
- w_down: bfloat16 [256, 256, 2048], P('expert', None, 'dp'), may hold values from -0.1875 to 0.1875
- cotangent: bfloat16 [4096, 2048], P('expert', 'dp'), may hold values from -6 to 6
Outputs:
- layer_out: bfloat16 [4096, 2048], P('expert', 'dp')
- d_tokens: bfloat16 [4096, 2048], P('expert', 'dp')
- d_up: float32 [256, 2048, 256], P('expert', 'dp')
- d_down: float32 [256, 256, 2048], P('expert', None, 'dp')
- d_sel: float32 [2048, 256], P('dp')
Inputs may be any that keep to these rules, and one draw needn't show every extreme that they name: `picks`: each row names 16 different experts. In each pass the 128 tokens of one device name any one expert at most 10 times, a bound that some block reaches. `halting`: the number of passes a token takes.
All inputs are finite; a program needn't handle non-finite values.
Results may differ from a plain program's by a relative error of at most 0.034.
Values may be sent and summed in bfloat16 or wider, within the bound.
No kernel may reach another device: no remote copies, remote signals or barrier semaphores. Data moves between devices by JAX's collectives and lax.ppermute only.
A program may use at most 128 MiB of HBM per device.

v0:
```python
import jax
import jax.numpy as jnp
from jax import lax
from jax.sharding import PartitionSpec as P

PASSES = 2


GELU_C = 0.7978845608028654
GELU_A = 0.044715


def gelu_tanh(pre_act):
    inner = GELU_C * (pre_act + GELU_A * pre_act * pre_act * pre_act)
    return 0.5 * pre_act * (1.0 + jnp.tanh(inner))


def gelu_slope(pre_act):
    inner = GELU_C * (pre_act + GELU_A * pre_act * pre_act * pre_act)
    tangent = jnp.tanh(inner)
    return 0.5 * (1.0 + tangent) + 0.5 * pre_act * (1.0 - tangent * tangent) * GELU_C * (
        1.0 + 3.0 * GELU_A * pre_act * pre_act
    )


def slot_table(chosen, experts, capacity):
    flat_ids = chosen.reshape(-1)
    total_picks = flat_ids.shape[0]
    sort_order = jnp.argsort(flat_ids, stable=True)
    sorted_ids = flat_ids[sort_order]
    counts = jnp.sum(
        (flat_ids[:, None] == jnp.arange(experts, dtype=jnp.int32)[None, :]).astype(jnp.int32),
        axis=0,
    )
    starts = jnp.cumsum(counts) - counts
    rank_in = jnp.arange(total_picks, dtype=jnp.int32) - starts[sorted_ids]
    slot_sorted = sorted_ids * capacity + rank_in
    slot_ids = jnp.zeros((total_picks,), jnp.int32).at[sort_order].set(slot_sorted)
    sources = (
        jnp.full((experts * capacity,), -1, jnp.int32)
        .at[slot_ids]
        .set(jnp.arange(total_picks, dtype=jnp.int32))
    )
    return (slot_ids, sources)


def per_device(tokens, picks, halting, w_sel, w_up, w_down, cotangent):
    tok_count, width_part = tokens.shape
    top_count = picks.shape[2]
    experts = w_sel.shape[1]
    capacity = 5 * tok_count * top_count // (4 * experts)
    expert_ids = jnp.arange(experts, dtype=jnp.int32)

    def to_experts(buffer):
        return lax.all_to_all(
            buffer.reshape(experts, capacity, width_part),
            "expert",
            split_axis=0,
            concat_axis=1,
            tiled=True,
        )

    def to_tokens(buffer):
        return lax.all_to_all(buffer, "expert", split_axis=1, concat_axis=0, tiled=True).reshape(
            experts * capacity, width_part
        )

    def width_sum(term_set):
        return lax.psum(term_set, "dp")

    def settle(partials, finish):
        total_sum = lax.psum(partials.astype(jnp.bfloat16), "dp").astype(jnp.float32)
        return (total_sum, finish(total_sum))

    current = tokens
    saved_pass = []
    for pass_id in range(PASSES):
        chosen = picks[pass_id]
        slot_ids, sources = slot_table(chosen, experts, capacity)
        logit_parts = jnp.take_along_axis(
            jnp.dot(current, w_sel, preferred_element_type=jnp.float32), chosen, axis=1
        )
        logits = width_sum(logit_parts)
        gate_prob = jax.nn.sigmoid(logits)
        active = (halting > pass_id).astype(jnp.float32)
        weights_tk = active[:, None] * gate_prob
        dispatch_usable = sources >= 0
        picked_rows = current[jnp.maximum(sources, 0) // top_count]
        received = to_experts(
            jnp.where(dispatch_usable[:, None], picked_rows, jnp.zeros((), jnp.bfloat16))
        )
        expert_partials = jnp.einsum(
            "erd,edh->erh", received, w_up, preferred_element_type=jnp.float32
        )
        pre_form, hidden = settle(
            expert_partials, lambda total_in: gelu_tanh(total_in).astype(jnp.bfloat16)
        )
        outputs = jnp.einsum(
            "erh,ehd->erd", hidden, w_down, preferred_element_type=jnp.float32
        ).astype(jnp.bfloat16)
        returned = to_tokens(outputs)
        per_pick = returned[slot_ids].reshape(tok_count, top_count, width_part)
        mixed_sum = jnp.sum(weights_tk[:, :, None] * per_pick.astype(jnp.float32), axis=1)
        saved_pass.append(
            (
                current,
                chosen,
                slot_ids,
                sources,
                gate_prob,
                active,
                weights_tk,
                per_pick,
                received,
                pre_form,
                hidden,
            )
        )
        current = (current.astype(jnp.float32) + mixed_sum).astype(jnp.bfloat16)
    layer_out = current
    cot_now = cotangent
    grad_up = jnp.zeros(w_up.shape, jnp.float32)
    grad_down = jnp.zeros(w_down.shape, jnp.float32)
    sel_grad = jnp.zeros(w_sel.shape, jnp.float32)
    for pass_id in reversed(range(PASSES)):
        (
            current,
            chosen,
            slot_ids,
            sources,
            gate_prob,
            active,
            weights_tk,
            per_pick,
            received,
            pre_form,
            hidden,
        ) = saved_pass[pass_id]
        cot_wide = cot_now.astype(jnp.float32)
        grad_pick = (
            (weights_tk[:, :, None] * cot_wide[:, None, :])
            .astype(jnp.bfloat16)
            .reshape(tok_count * top_count, width_part)
        )
        usable = sources >= 0
        grad_slots = jnp.where(
            usable[:, None], grad_pick[jnp.maximum(sources, 0)], jnp.zeros((), jnp.bfloat16)
        )
        score_parts = (
            jnp.sum(cot_wide[:, None, :] * per_pick.astype(jnp.float32), axis=2) * active[:, None]
        )
        score_grad = width_sum(score_parts)
        grad_in = to_experts(grad_slots)
        grad_part = jnp.einsum("erd,ehd->erh", grad_in, w_down, preferred_element_type=jnp.float32)
        act_slope = gelu_slope(pre_form)
        unused_sum, grad_pre = settle(
            grad_part, lambda total_in: (total_in * act_slope).astype(jnp.bfloat16)
        )
        grad_down = grad_down + jnp.einsum(
            "erh,erd->ehd", hidden, grad_in, preferred_element_type=jnp.float32
        )
        grad_up = grad_up + jnp.einsum(
            "erd,erh->edh", received, grad_pre, preferred_element_type=jnp.float32
        )
        grad_rows = jnp.einsum(
            "erh,edh->erd", grad_pre, w_up, preferred_element_type=jnp.float32
        ).astype(jnp.bfloat16)
        grad_back = to_tokens(grad_rows)
        grad_picks = grad_back[slot_ids].reshape(tok_count, top_count, width_part)
        logit_grad = score_grad * gate_prob * (1.0 - gate_prob)
        pick_table = jnp.sum(
            logit_grad[:, :, None]
            * (chosen[:, :, None] == expert_ids[None, None, :]).astype(jnp.float32),
            axis=1,
        ).astype(jnp.bfloat16)
        sel_grad = sel_grad + jnp.dot(current.T, pick_table, preferred_element_type=jnp.float32)
        router_back = jnp.dot(pick_table, w_sel.T, preferred_element_type=jnp.float32)
        cot_now = (cot_wide + jnp.sum(grad_picks.astype(jnp.float32), axis=1) + router_back).astype(
            jnp.bfloat16
        )
    sel_total = lax.psum(sel_grad.astype(jnp.bfloat16), "expert").astype(jnp.float32)
    return (layer_out, cot_now, grad_up, grad_down, sel_total)


def solution(mesh):
    in_specs = (
        P("expert", "dp"),
        P(None, "expert", None),
        P("expert"),
        P("dp", None),
        P("expert", "dp", None),
        P("expert", None, "dp"),
        P("expert", "dp"),
    )
    out_specs = (
        P("expert", "dp"),
        P("expert", "dp"),
        P("expert", "dp", None),
        P("expert", None, "dp"),
        P("dp", None),
    )
    return jax.shard_map(
        per_device, mesh=mesh, in_specs=in_specs, out_specs=out_specs, check_vma=False
    )
```

profile of v0, /device:TPU:1, one launch (start us, length us, event | category | flops | bytes accessed | tf_op | source)
XLA Modules:
  0.0 1014.8 jit_solution(6130546037285196024)
XLA Ops:
  14.3 11.8 %gather_fusion = s32[2048]{0:T(1024)S(1)} fusion(s32[2048]{0:T(1024)S(1)} %reshape_squeeze.6, s32[2048]{0:T(1024)S(1)} %get-tuple-element.26), kind=kCustom, calls=%fused_computation.2 | custom fusion | bytes 24576 | tf_op jit(solution)/shard_map/gather | solution.py:30
  26.1 13.1 %gather_fusion.1 = s32[2048]{0:T(1024)S(1)} fusion(s32[256]{0:T(256)S(1)} %bitcast_subtract_fusion.1, s32[2048]{0:T(1024)S(1)} %broadcast_clamp_fusion.3), kind=kCustom, calls=%fused_computation.3 | custom fusion | bytes 24576 | tf_op jit(solution)/shard_map/gather | solution.py:36
  39.3 8.0 scatter_custom_fusion
  47.4 8.1 scatter_custom_fusion.1
  56.2 8.2 gather_fusion.2
  64.4 5.9 gather.55
  73.0 60.3 %all_to_all.132 = bf16[256,10,512]{2,1,0:T(8,128)(2,1)S(1)} all-to-all(bf16[256,10,512]{2,1,0:T(8,128)(2,1)S(1)} %broadcast_select_fusion.3), channel_id=1, replica_groups=mesh['dp'=4,'expert'=32] {'expert'}, dimensions={0} | all-to-all | bytes 5242880 | tf_op jit(solution)/shard_map/all_to_all | solution.py:55
  145.7 11.8 %gather_fusion.4 = s32[2048]{0:T(1024)S(1)} fusion(s32[2048]{0:T(1024)S(1)} %reshape_squeeze.7, s32[2048]{0:T(1024)S(1)} %get-tuple-element.22), kind=kCustom, calls=%fused_computation.6 | custom fusion | bytes 24576 | tf_op jit(solution)/shard_map/gather | solution.py:30
  157.6 26.5 %all-reduce.7.cloned.1.call-done = bf16[8,320,256]{2,1,0:T(8,128)(2,1)} async-done(((bf16[8,320,256]{2,1,0:T(8,128)(2,1)}), bf16[8,320,256]{2,1,0:T(8,128)(2,1)}) %all-reduce.7.cloned.1.call-update) | async-done | bytes 1310736 | tf_op jit(solution)/shard_map/psum | solution.py:72
  189.5 9.0 all-to-all-start.1
  198.6 13.1 %gather_fusion.5 = s32[2048]{0:T(1024)S(1)} fusion(s32[256]{0:T(256)S(1)} %bitcast_subtract_fusion, s32[2048]{0:T(1024)S(1)} %broadcast_clamp_fusion.2), kind=kCustom, calls=%fused_computation.7 | custom fusion | bytes 24576 | tf_op jit(solution)/shard_map/gather | solution.py:36
  211.8 8.0 scatter_custom_fusion.2
  219.9 8.2 scatter_custom_fusion.3
  228.6 16.6 %gather_fusion.12 = f32[2048]{0:T(1024)S(1)} fusion(f32[128,256]{1,0:T(8,128)S(1)} %fusion.91, s32[2048]{0:T(1024)S(1)} %reshape.344), kind=kCustom, calls=%fused_computation.clone | custom fusion | bytes 32768 | tf_op jit(solution)/shard_map/jit(take_along_axis)/gather | solution.py:80
  245.4 12.7 %psum.63 = f32[128,16]{1,0:T(8,128)S(1)} all-reduce(f32[128,16]{1,0:T(8,128)S(1)} %and_select_fusion.1), channel_id=1, replica_groups=mesh['dp'=4,'expert'=32] {'dp'}, use_global_device_ids=true, to_apply=%region_0.2 | all-reduce | flops 2048 | bytes 16384 | tf_op jit(solution)/shard_map/psum | solution.py:69
  258.3 5.2 copy.82
  263.5 6.1 reshape.168
  269.6 11.3 %gather_fusion.3 = bf16[2048,512]{1,0:T(8,128)(2,1)} fusion(bf16[2560,512]{1,0:T(8,128)(2,1)} %reshape.168, s32[2048]{0:T(1024)S(1)} %get-tuple-element.24), kind=kCustom, calls=%fused_computation.5 | custom fusion | bytes 4202496 | tf_op jit(solution)/shard_map/gather | solution.py:102
  283.7 8.2 gather_fusion.6
  291.9 5.9 gather.61
  300.5 61.8 %all_to_all.133 = bf16[256,10,512]{2,1,0:T(8,128)(2,1)S(1)} all-to-all(bf16[256,10,512]{2,1,0:T(8,128)(2,1)S(1)} %broadcast_select_fusion.1), channel_id=1, replica_groups=mesh['dp'=4,'expert'=32] {'expert'}, dimensions={0} | all-to-all | bytes 5242880 | tf_op jit(solution)/shard_map/all_to_all | solution.py:55
  368.7 42.6 %all-reduce.9.cloned.1.call-done = bf16[8,320,256]{2,1,0:T(8,128)(2,1)} async-done(((bf16[8,320,256]{2,1,0:T(8,128)(2,1)}), bf16[8,320,256]{2,1,0:T(8,128)(2,1)}) %all-reduce.9.cloned.1.call-update) | async-done | bytes 1310736 | tf_op jit(solution)/shard_map/psum | solution.py:72
  416.7 9.1 all-to-all-start.3
  426.2 16.6 %gather_fusion.13 = f32[2048]{0:T(1024)S(1)} fusion(f32[128,256]{1,0:T(8,128)S(1)} %fusion.92, s32[2048]{0:T(1024)S(1)} %reshape.349), kind=kCustom, calls=%fused_computation.1.clone | custom fusion | bytes 32768 | tf_op jit(solution)/shard_map/jit(take_along_axis)/gather | solution.py:80
  442.9 16.8 %all-to-all-done.3 = bf16[8,320,512]{2,0,1:T(8,128)(2,1)} async-done(((bf16[8,320,512]{2,0,1:T(8,128)(2,1)}), bf16[8,320,512]{2,0,1:T(8,128)(2,1)}, u32[]{:S(2)}, u32[]{:S(2)}) %all-to-all-start.3) | async-done | bytes 2621472 | tf_op jit(solution)/shard_map/all_to_all | solution.py:64
  465.0 6.1 reshape.171
  471.1 11.3 %gather_fusion.7 = bf16[2048,512]{1,0:T(8,128)(2,1)} fusion(bf16[2560,512]{1,0:T(8,128)(2,1)} %reshape.171, s32[2048]{0:T(1024)S(1)} %get-tuple-element.20), kind=kCustom, calls=%fused_computation.9 | custom fusion | bytes 4202496 | tf_op jit(solution)/shard_map/gather | solution.py:102
  485.2 15.0 %all-reduce = (f32[128,16]{1,0:T(8,128)}, f32[128,16]{1,0:T(8,128)}) all-reduce(f32[128,16]{1,0:T(8,128)S(1)} %and_select_fusion, f32[128,16]{1,0:T(8,128)} %broadcast_multiply_fusion), channel_id=1, replica_groups=mesh['dp'=4,'expert'=32] {'dp'}, use_global_device_ids=true, to_apply=%region_9.11 | all-reduce | flops 4096 | bytes 32768 | tf_op jit(solution)/shard_map/psum | solution.py:69
  502.9 10.2 %gather_fusion.8 = bf16[2560,512]{1,0:T(8,128)(2,1)} fusion(bf16[2048,512]{1,0:T(8,128)(2,1)} %fusion.5, s32[3072]{0:T(1024)S(1)} %get-tuple-element.32), kind=kCustom, calls=%fused_computation.10 | custom fusion | bytes 5253120 | tf_op jit(solution)/shard_map/gather | solution.py:147
  513.1 5.9 gather.64
  521.6 58.4 %all_to_all.134 = bf16[256,10,512]{2,1,0:T(8,128)(2,1)S(1)} all-to-all(bf16[256,10,512]{2,1,0:T(8,128)(2,1)S(1)} %broadcast_select_fusion), channel_id=1, replica_groups=mesh['dp'=4,'expert'=32] {'expert'}, dimensions={0} | all-to-all | bytes 5242880 | tf_op jit(solution)/shard_map/all_to_all | solution.py:55
  586.3 42.7 %all-reduce.11.cloned.1.call-done = bf16[8,320,256]{2,1,0:T(8,128)(2,1)} async-done(((bf16[8,320,256]{2,1,0:T(8,128)(2,1)}), bf16[8,320,256]{2,1,0:T(8,128)(2,1)}) %all-reduce.11.cloned.1.call-update) | async-done | bytes 1310736 | tf_op jit(solution)/shard_map/psum | solution.py:72
  636.4 9.3 all-to-all-start.5
  646.7 32.9 %all-to-all-done.5 = bf16[8,320,512]{2,0,1:T(8,128)(2,1)} async-done(((bf16[8,320,512]{2,0,1:T(8,128)(2,1)}), bf16[8,320,512]{2,0,1:T(8,128)(2,1)}, u32[]{:S(2)}, u32[]{:S(2)}) %all-to-all-start.5) | async-done | bytes 2621472 | tf_op jit(solution)/shard_map/all_to_all | solution.py:64
  684.8 6.1 reshape.172
  690.9 11.3 %gather_fusion.9 = bf16[2048,512]{1,0:T(8,128)(2,1)} fusion(bf16[2560,512]{1,0:T(8,128)(2,1)} %reshape.172, s32[2048]{0:T(1024)S(1)} %get-tuple-element.20), kind=kCustom, calls=%fused_computation.11 | custom fusion | bytes 4202496 | tf_op jit(solution)/shard_map/gather | solution.py:169
  706.7 10.2 %gather_fusion.10 = bf16[2560,512]{1,0:T(8,128)(2,1)} fusion(bf16[2048,512]{1,0:T(8,128)(2,1)} %fusion.4, s32[3072]{0:T(1024)S(1)} %copy-done.13), kind=kCustom, calls=%fused_computation.12 | custom fusion | bytes 5253120 | tf_op jit(solution)/shard_map/gather | solution.py:147
  716.9 5.9 gather.67
  726.8 5.4 all-to-all-start.6
  736.8 47.6 %all-to-all-done.6 = bf16[256,10,512]{2,1,0:T(8,128)(2,1)} async-done(((bf16[256,10,512]{2,1,0:T(8,128)(2,1)}), bf16[256,10,512]{2,1,0:T(8,128)(2,1)}, u32[]{:S(2)}, u32[]{:S(2)}) %all-to-all-start.6) | async-done | bytes 2621472 | tf_op jit(solution)/shard_map/all_to_all | solution.py:55
  796.8 13.4 %psum.70 = f32[128,16]{1,0:T(8,128)S(1)} all-reduce(f32[128,16]{1,0:T(8,128)S(1)} %broadcast_multiply_fusion.2), channel_id=1, replica_groups=mesh['dp'=4,'expert'=32] {'dp'}, use_global_device_ids=true, to_apply=%region_26.28 | all-reduce | flops 2048 | bytes 16384 | tf_op jit(solution)/shard_map/psum | solution.py:69
  812.0 27.9 %all-reduce.13.cloned.1.call-done = bf16[8,320,256]{2,1,0:T(8,128)(2,1)} async-done(((bf16[8,320,256]{2,1,0:T(8,128)(2,1)}), bf16[8,320,256]{2,1,0:T(8,128)(2,1)}) %all-reduce.13.cloned.1.call-update) | async-done | bytes 1310736 | tf_op jit(solution)/shard_map/psum | solution.py:72
  847.3 9.4 all-to-all-start.7
  856.7 7.9 fusion.36
  864.6 100.6 %all-reduce.15.cloned.1.call-done = bf16[512,256]{1,0:T(8,128)(2,1)} async-done(((bf16[512,256]{1,0:T(8,128)(2,1)}), bf16[512,256]{1,0:T(8,128)(2,1)}) %all-reduce.15.cloned.1.call-update) | async-done | bytes 262160 | tf_op jit(solution)/shard_map/psum | solution.py:181
  976.3 5.6 fusion.44
  987.0 6.1 reshape.173
  993.2 11.3 %gather_fusion.11 = bf16[2048,512]{1,0:T(8,128)(2,1)} fusion(bf16[2560,512]{1,0:T(8,128)(2,1)} %reshape.173, s32[2048]{0:T(1024)S(1)} %get-tuple-element.24), kind=kCustom, calls=%fused_computation.13 | custom fusion | bytes 4202496 | tf_op jit(solution)/shard_map/gather | solution.py:169
  (154 shorter events, 134.1 us)
Async XLA Ops:
  7.2 176.9 %copy-start = (bf16[8,256,512]{2,1,0:T(8,128)(2,1)S(1)}, bf16[8,256,512]{2,1,0:T(8,128)(2,1)}, u32[]{:S(2)}) copy-start(bf16[8,256,512]{2,1,0:T(8,128)(2,1)} %param.14) | copy-start | bytes 6291460
  7.2 176.9 %all-reduce.7.cloned.1.call-start = ((), (), s32[]{:S(2)}) async-start(), calls=%async_computation.8 | async-start | bytes 2621440 | tf_op jit(solution)/shard_map/psum | solution.py:72
  26.1 30.1 %copy-start.1 = (bf16[128,512]{1,0:T(8,128)(2,1)S(1)}, bf16[128,512]{1,0:T(8,128)(2,1)}, u32[]{:S(2)}) copy-start(bf16[128,512]{1,0:T(8,128)(2,1)} %param.9) | copy-start | bytes 393220
  133.3 4.3 copy-start.14
  136.1 1.5 copy-start.5
  189.5 68.8 %all-to-all-start.1 = ((bf16[8,320,512]{2,0,1:T(8,128)(2,1)}), bf16[8,320,512]{2,0,1:T(8,128)(2,1)}, u32[]{:S(2)}, u32[]{:S(2)}) async-start(bf16[8,320,512]{2,0,1:T(8,128)(2,1)} %copy.81), calls=%async_computation.1 | async-start | bytes 5242880 | tf_op jit(solution)/shard_map/all_to_all | solution.py:64
  198.5 212.8 %all-reduce.9.cloned.1.call-start = ((), (), s32[]{:S(2)}) async-start(), calls=%async_computation.9 | async-start | bytes 2621440 | tf_op jit(solution)/shard_map/psum | solution.py:72
  198.6 29.8 %copy-start.4 = (bf16[512,256]{1,0:T(8,128)(2,1)S(1)}, bf16[512,256]{1,0:T(8,128)(2,1)}, u32[]{:S(2)}) copy-start(bf16[512,256]{1,0:T(8,128)(2,1)} %param.12) | copy-start | bytes 786436
  228.6 29.6 %copy-start.18 = (s32[128]{0:T(128)S(1)}, s32[128]{0:T(128)}, u32[]{:S(2)}) copy-start(s32[128]{0:T(128)} %param.11) | copy-start | bytes 1540
  362.3 4.3 copy-start.15
  365.0 1.5 copy-start.7
  416.7 9.3 copy-start.12
  416.7 43.1 %all-to-all-start.3 = ((bf16[8,320,512]{2,0,1:T(8,128)(2,1)}), bf16[8,320,512]{2,0,1:T(8,128)(2,1)}, u32[]{:S(2)}, u32[]{:S(2)}) async-start(bf16[8,320,512]{2,0,1:T(8,128)(2,1)} %copy.87), calls=%async_computation.3 | async-start | bytes 5242880 | tf_op jit(solution)/shard_map/all_to_all | solution.py:64
  425.8 203.2 %all-reduce.11.cloned.1.call-start = ((), (), s32[]{:S(2)}) async-start(), calls=%async_computation.10 | async-start | bytes 2621440 | tf_op jit(solution)/shard_map/psum | solution.py:72
  501.2 11.9 %copy-start.10 = (f32[128,16]{1,0:T(8,128)}, f32[128,16]{1,0:T(8,128)S(1)}, u32[]{:S(2)}) copy-start(f32[128,16]{1,0:T(8,128)S(1)} %get-tuple-element.13) | copy-start | bytes 24580
  582.8 1.5 copy-start.2
  636.4 43.1 %all-to-all-start.5 = ((bf16[8,320,512]{2,0,1:T(8,128)(2,1)}), bf16[8,320,512]{2,0,1:T(8,128)(2,1)}, u32[]{:S(2)}, u32[]{:S(2)}) async-start(bf16[8,320,512]{2,0,1:T(8,128)(2,1)} %copy.92), calls=%async_computation.5 | async-start | bytes 5242880 | tf_op jit(solution)/shard_map/all_to_all | solution.py:64
  646.7 58.1 %copy-start.11 = (bf16[128,256]{1,0:T(8,128)(2,1)}, bf16[128,256]{1,0:T(8,128)(2,1)S(1)}, u32[]{:S(2)}) copy-start(bf16[128,256]{1,0:T(8,128)(2,1)S(1)} %select_reduce_fusion.1) | copy-start | bytes 196612
  702.2 4.5 copy-start.13
  726.8 57.7 %all-to-all-start.6 = ((bf16[256,10,512]{2,1,0:T(8,128)(2,1)}), bf16[256,10,512]{2,1,0:T(8,128)(2,1)}, u32[]{:S(2)}, u32[]{:S(2)}) async-start(bf16[256,10,512]{2,1,0:T(8,128)(2,1)} %broadcast_select_fusion.2), calls=%async_computation.6 | async-start | bytes 8388608 | tf_op jit(solution)/shard_map/all_to_all | solution.py:55
  732.2 107.7 %all-reduce.13.cloned.1.call-start = ((), (), s32[]{:S(2)}) async-start(), calls=%async_computation.11 | async-start | bytes 2621440 | tf_op jit(solution)/shard_map/psum | solution.py:72
  789.4 1.5 copy-start.8
  793.0 172.3 %all-reduce.15.cloned.1.call-start = ((), (), s32[]{:S(2)}) async-start(), calls=%async_computation.12 | async-start | bytes 524288 | tf_op jit(solution)/shard_map/psum | solution.py:181
  847.3 134.6 %all-to-all-start.7 = ((bf16[8,320,512]{2,0,1:T(8,128)(2,1)}), bf16[8,320,512]{2,0,1:T(8,128)(2,1)}, u32[]{:S(2)}, u32[]{:S(2)}) async-start(bf16[8,320,512]{2,0,1:T(8,128)(2,1)} %copy.97), calls=%async_computation.7 | async-start | bytes 5242880 | tf_op jit(solution)/shard_map/all_to_all | solution.py:64
  967.0 4.7 copy-start.3
  967.0 4.7 copy-start.9
  971.7 4.6 copy-start.6
  971.7 4.5 copy-start.16
  971.7 4.5 copy-start.17
  971.7 4.5 copy-start.19
Sparse Core Ops, SparseCore 0:
  139.8 44.2 all-reduce.6
  368.8 42.4 all-reduce.8
  586.5 42.4 all-reduce.10
  793.1 46.7 all-reduce.12
  843.5 121.6 all-reduce.14
where the time goes:
time: 1020 us; the launch traced here: 1010 us
  waiting for transfers between devices  338 us (33%)
  local copies, waits for them, and re-layouts  300 us (29%)
  blocking collectives  222 us (22%)
  other arithmetic  49.9 us (5%)
  matrix products  48.4 us (5%)
  starting transfers between devices  42.4 us (4%)
  between operations  14.8 us (1%)
    all_to_all x3, blocking collectives, to_experts(): lax.all_to_all(buffer.reshape(experts, capacity, width_part), 'expert', s...  181 us
    psum x4, waiting for transfers between devices, settle(): lax.psum(partials.astype(jnp.bfloat16), 'dp').astype(jnp.float32)  140 us
    psum x1, waiting for transfers between devices, per_device(): lax.psum(sel_grad.astype(jnp.bfloat16), 'expert').astype(jnp.float32)  101 us
    all_to_all x4, waiting for transfers between devices, to_tokens(): lax.all_to_all(buffer, 'expert', split_axis=1, concat_axis=0, tiled=True)  49.7 us
    all_to_all x1, waiting for transfers between devices, to_experts(): lax.all_to_all(buffer.reshape(experts, capacity, width_part), 'expert', s...  47.6 us
    psum x3, blocking collectives, width_sum(): return lax.psum(term_set, 'dp')  41.1 us
    all_to_all x4, starting transfers between devices, to_tokens(): lax.all_to_all(buffer, 'expert', split_axis=1, concat_axis=0, tiled=True)  36.8 us
    gather x6, local copies, waits for them, and re-layouts, per_device(): jnp.take_along_axis(jnp.dot(current, w_sel, preferred_element_type=jnp.fl...  33.6 us
  transfers between devices with their start and end apart: 10, of which 8 were waited for; matrix products, arithmetic and copies ran while one was open for 12% of the time, Pallas kernels for 0%

commit v1 on v0

v1 whole, which is shorter than its diff:
```python
import jax
import jax.numpy as jnp
from jax import lax
from jax.experimental import pallas as pl
from jax.experimental.pallas import tpu as pltpu
from jax.sharding import PartitionSpec as P

BF = jnp.bfloat16
F32 = jnp.float32
GELU_C = 0.7978845608028654
GELU_A = 0.044715

TOK = 128
HALF = 256
HID = 256
NE = 8
CAP = 10
GRP = 8
GROUPS = 4
GTOK = GRP * TOK
GSLOT = GRP * CAP
ESLOT = GROUPS * GSLOT
OWN = 2 * ESLOT
EXT = 16
VMEM = pl.BlockSpec(memory_space=pltpu.VMEM)
SMEM = pl.BlockSpec(memory_space=pltpu.SMEM)


def dev(x, z, c):
    return (x * 4 + z) * 2 + c


PLACES = [(x, z, c) for x in range(4) for z in range(4) for c in range(2)]
SWAP = [(dev(x, z, c), dev(x, z, 1 - c)) for x, z, c in PLACES]


def along(axis, step):
    pairs = []
    for x, z, c in PLACES:
        if (axis + c) % 2 == 1:
            pairs.append((dev(x, z, c), dev((x + step) % 4, z, c)))
        else:
            pairs.append((dev(x, z, c), dev(x, (z + step) % 4, c)))
    return pairs


def hop(value, axis, step):
    return lax.ppermute(value, "expert", along(axis, step % 4))


def swap(value):
    return lax.ppermute(value, "expert", SWAP)


def hop_dp(value, step):
    return lax.ppermute(value, "dp", [(y, (y + step) % 4) for y in range(4)])


def call(body, outs, ins, flops=0, bytes_accessed=1 << 20, scratch=(), smem=0, limit=56):
    return pl.pallas_call(
        body,
        out_shape=outs,
        in_specs=[SMEM] * smem + [VMEM] * (len(ins) - smem),
        out_specs=jax.tree.map(lambda _: VMEM, outs),
        scratch_shapes=list(scratch),
        compiler_params=pltpu.CompilerParams(vmem_limit_bytes=limit * 1024 * 1024),
        cost_estimate=pl.CostEstimate(flops=flops, bytes_accessed=bytes_accessed, transcendentals=0),
    )(*ins)


def shape(dims, dtype):
    return jax.ShapeDtypeStruct(dims, dtype)


def mm(a, b):
    return lax.dot_general(a, b, (((1,), (0,)), ((), ())), preferred_element_type=F32)


def mm_nt(a, b):
    return lax.dot_general(a, b, (((1,), (1,)), ((), ())), preferred_element_type=F32)


def mm_tn(a, b):
    return lax.dot_general(a, b, (((0,), (0,)), ((), ())), preferred_element_type=F32)


def routing_body(eid_ref, *refs):
    own, (v_ref, vt_ref) = refs[:4], refs[4:]
    eid = eid_ref[:, :]
    marks = []
    for g in range(GROUPS):
        for j in range(GRP):
            named = own[g][GTOK + 16 * j : GTOK + 16 * j + 16, :].astype(F32)
            mark = jnp.zeros((NE, 256), F32)
            for k in range(16):
                mark = jnp.where(named[k : k + 1, :] == eid, 1.0, mark)
            marks.append(mark)
    before = lax.broadcasted_iota(jnp.int32, (TOK, TOK), 0) < lax.broadcasted_iota(jnp.int32, (TOK, TOK), 1)
    before = jnp.where(before, 1.0, 0.0).astype(BF)
    for p in range(2):
        stacked = jnp.concatenate([m[:, p * TOK : (p + 1) * TOK] for m in marks], axis=0)
        rank = mm(stacked.astype(BF), before)
        for g in range(GROUPS):
            rows = []
            for j in range(GRP):
                at = (g * GRP + j) * NE
                rows.append(jnp.where(stacked[at : at + NE] > 0, rank[at : at + NE] + float(CAP * j), -1.0))
            v = jnp.concatenate(rows, axis=1)
            v_ref[p, g] = v
            padded = jnp.concatenate([v, jnp.zeros((TOK - NE, GTOK), F32)], axis=0)
            vt_ref[p, g] = padded.T.astype(BF)


def gather_rows(v_ref, own, oth, x_ref):
    slot = lax.broadcasted_iota(jnp.int32, (GSLOT, GTOK), 0).astype(F32)
    for g in range(GROUPS):
        v = v_ref[g]
        pick = jnp.concatenate([jnp.where(slot == v[e : e + 1, :], 1.0, 0.0).astype(BF) for e in range(NE)], axis=0)
        near = own[g][0:GTOK, :]
        far = jnp.concatenate(
            [
                oth[d1][(g * 2 + 1 - dc) * TOK : (g * 2 + 2 - dc) * TOK, :]
                for d1 in range(4)
                for dc in range(2)
            ],
            axis=0,
        )
        for h, source in enumerate((near, far)):
            rows = mm(pick, source).astype(BF)
            for e in range(NE):
                x_ref[e, g * GSLOT : (g + 1) * GSLOT, h * HALF : (h + 1) * HALF] = rows[e * GSLOT : (e + 1) * GSLOT]


def halves(sc_ref):
    core = sc_ref[1]
    return (
        pl.ds(pl.multiple_of(core * HALF, HALF), HALF),
        pl.ds(pl.multiple_of((1 - core) * HALF, HALF), HALF),
    )


def expert_at(sc_ref, e):
    return lax.rem(2 * sc_ref[0] + e, NE)


def up_body(sc_ref, v_ref, w_up_ref, sel_ref, *refs):
    own, oth, x_ref, parts = refs[0:4], refs[4:8], refs[8], refs[9:13]
    gather_rows(v_ref, own, oth, x_ref)
    first, second = halves(sc_ref)
    sel = sel_ref[:, :]
    lane_pad = jnp.zeros((1, 192), F32)
    for dy in range(4):
        heads, tails = [], []
        for i in range(2):
            e = 2 * dy + i
            at = expert_at(sc_ref, e)
            rows = x_ref[e]
            total = mm(rows[:, :HALF], w_up_ref[at, first, :]) + mm(rows[:, HALF:], w_up_ref[at, second, :])
            parts[dy][i * ESLOT : (i + 1) * ESLOT, :] = total.astype(BF)
            logit = mm_nt(sel, rows)[e : e + 1, :]
            heads.append(logit[:, :256])
            tails.append(jnp.concatenate([logit[:, 256:], lane_pad], axis=1))
        logits = jnp.concatenate(heads + tails, axis=0)
        high = logits.astype(BF).astype(F32)
        low = logits - high
        parts[dy][OWN:, :] = jnp.concatenate([high, low, jnp.zeros((8, 256), F32)], axis=0).astype(BF)


def down_grad_body(sc_ref, v_ref, w_down_ref, *refs):
    own, oth, x_ref, parts = refs[0:4], refs[4:8], refs[8], refs[9:13]
    gather_rows(v_ref, own, oth, x_ref)
    first, second = halves(sc_ref)
    for e in range(NE):
        at = expert_at(sc_ref, e)
        rows = x_ref[e]
        total = mm_nt(rows[:, :HALF], w_down_ref[at, :, first]) + mm_nt(rows[:, HALF:], w_down_ref[at, :, second])
        parts[e // 2][(e % 2) * ESLOT : (e % 2 + 1) * ESLOT, :] = total.astype(BF)


def as_columns(rows):
    turned = jnp.concatenate([rows, jnp.zeros((TOK - rows.shape[0], 256), F32)], axis=0).T
    return jnp.concatenate([turned[:, 0:1], turned[:64, 2:3], turned[:, 1:2], turned[:64, 3:4]], axis=0)


def as_rows(column):
    wide = jnp.broadcast_to(column, (OWN, TOK))
    lane = lax.broadcasted_iota(jnp.int32, (256, TOK), 1)
    pad = jnp.zeros((192, TOK), F32)
    pieces = (
        wide[0:256],
        wide[ESLOT : ESLOT + 256],
        jnp.concatenate([wide[256:ESLOT], pad], axis=0),
        jnp.concatenate([wide[ESLOT + 256 :], pad], axis=0),
    )
    mixed = jnp.zeros((256, TOK), F32)
    for i, piece in enumerate(pieces):
        mixed = jnp.where(lane == i, piece, mixed)
    return mixed.T[:EXT]


def settle_body(p0, p1, p2, p3, hid_ref, pre_ref, gate_ref):
    def total(lo, hi):
        return sum(p[lo:hi, :].astype(F32) for p in (p0, p1, p2, p3))

    extra = total(OWN, OWN + EXT)
    gate = jax.nn.sigmoid(as_columns(extra[0:4] + extra[4:8]))
    pre = total(0, OWN)
    pre_ref[:, :] = pre
    gate_ref[:, :] = jnp.broadcast_to(gate, (OWN, TOK))
    inner = GELU_C * (pre + GELU_A * pre * pre * pre)
    hid_ref[:, :] = (gate * (0.5 * pre * (1.0 + jnp.tanh(inner)))).astype(BF)


def settle_grad_body(p0, p1, p2, p3, pre_ref, gate_ref, grad_ref):
    total = sum(p[:, :].astype(F32) for p in (p0, p1, p2, p3))
    pre = pre_ref[:, :]
    gate = gate_ref[:, 0:1]
    tangent = jnp.tanh(GELU_C * (pre + GELU_A * pre * pre * pre))
    hidden = (0.5 * pre * (1.0 + tangent)).astype(BF).astype(F32)
    slope = 0.5 * (1.0 + tangent) + 0.5 * pre * (1.0 - tangent * tangent) * GELU_C * (1.0 + 3.0 * GELU_A * pre * pre)
    score = jnp.sum(hidden * total, axis=1, keepdims=True)
    grad_ref[0:OWN, :] = (gate * total * slope).astype(BF)
    grad_ref[OWN:, :] = as_rows(score * gate * (1.0 - gate)).astype(BF)


def scatter_rows(vt_ref, out_ref, own_ref, oth_ref):
    at_lane = lax.broadcasted_iota(jnp.int32, (TOK, NE * GSLOT), 1)
    at_row = lax.broadcasted_iota(jnp.int32, (TOK, NE * GSLOT), 0)
    spread = jnp.where((at_lane >= at_row * GSLOT) & (at_lane < (at_row + 1) * GSLOT), 1.0, 0.0).astype(BF)
    lane = lax.broadcasted_iota(jnp.int32, (1, NE * GSLOT), 1)
    slot = lax.rem(lane, GSLOT).astype(F32)
    for g in range(GROUPS):
        put = jnp.where(mm(vt_ref[g], spread) == slot, 1.0, 0.0).astype(BF)
        far = mm(put, out_ref[g, :, HALF:]).astype(BF)
        for d1 in range(4):
            for dc in range(2):
                j = d1 * 2 + dc
                to = (d1 * 8 + g * 2 + 1 - dc) * TOK
                oth_ref[to : to + TOK, :] = far[j * TOK : (j + 1) * TOK]
        own_ref[g * GTOK : (g + 1) * GTOK, :] = mm(put, out_ref[g, :, :HALF]).astype(BF)


def down_body(sc_ref, vt_ref, w_down_ref, h0, h1, h2, h3, own_ref, oth_ref, out_ref):
    hid = (h0, h1, h2, h3)
    first, second = halves(sc_ref)
    for e in range(NE):
        at = expert_at(sc_ref, e)
        rows = hid[e // 2][(e % 2) * ESLOT : (e % 2 + 1) * ESLOT, :]
        for h, cols in enumerate((first, second)):
            out = mm(rows, w_down_ref[at, :, cols]).astype(BF)
            for g in range(GROUPS):
                out_ref[g, e * GSLOT : (e + 1) * GSLOT, h * HALF : (h + 1) * HALF] = out[g * GSLOT : (g + 1) * GSLOT]
    scatter_rows(vt_ref, out_ref, own_ref, oth_ref)


def logit_rows(grads):
    rows = []
    for piece in grads:
        extra = piece[OWN:, :].astype(F32)
        for i in range(2):
            rows.append(jnp.concatenate([extra[i : i + 1, :], extra[2 + i : 3 + i, :64]], axis=1))
    return jnp.concatenate(rows, axis=0)


def up_grad_body(sc_ref, vt_ref, w_up_ref, sel_ref, h0, h1, h2, h3, own_ref, oth_ref, out_ref):
    grads = (h0, h1, h2, h3)
    first, second = halves(sc_ref)
    sel = sel_ref[:, :].astype(F32)
    rows = logit_rows(grads)
    rows = jnp.concatenate([rows, jnp.zeros((NE, 64), F32)], axis=1)
    columns = jnp.concatenate([rows, jnp.zeros((TOK - NE, 384), F32)], axis=0).T
    for e in range(NE):
        at = expert_at(sc_ref, e)
        grad = grads[e // 2][(e % 2) * ESLOT : (e % 2 + 1) * ESLOT, :]
        logit_grad = columns[:ESLOT, e : e + 1]
        for h, cols in enumerate((first, second)):
            out = mm_nt(grad, w_up_ref[at, cols, :])
            out = (out + logit_grad * sel[e : e + 1, h * HALF : (h + 1) * HALF]).astype(BF)
            for g in range(GROUPS):
                out_ref[g, e * GSLOT : (e + 1) * GSLOT, h * HALF : (h + 1) * HALF] = out[g * GSLOT : (g + 1) * GSLOT]
    scatter_rows(vt_ref, out_ref, own_ref, oth_ref)


def d_down_body(sc_ref, c0_ref, c1_ref, *refs):
    hid, d_ref = (refs[0:4], refs[4:8]), refs[8]
    first, second = halves(sc_ref)
    for e in range(NE):
        at = expert_at(sc_ref, e)
        span = slice((e % 2) * ESLOT, (e % 2 + 1) * ESLOT)
        for h, cols in enumerate((first, second)):
            part = slice(h * HALF, (h + 1) * HALF)
            d_ref[at, :, cols] = mm_tn(hid[0][e // 2][span, :], c0_ref[e, :, part]) + mm_tn(
                hid[1][e // 2][span, :], c1_ref[e, :, part]
            )


def d_up_body(sc_ref, x0_ref, x1_ref, *refs):
    grads, d_ref, sel_ref = (refs[0:4], refs[4:8]), refs[8], refs[9]
    first, second = halves(sc_ref)
    rows = [logit_rows(grads[p]).astype(BF) for p in range(2)]
    for e in range(NE):
        at = expert_at(sc_ref, e)
        span = slice((e % 2) * ESLOT, (e % 2 + 1) * ESLOT)
        for h, cols in enumerate((first, second)):
            part = slice(h * HALF, (h + 1) * HALF)
            d_ref[at, cols, :] = mm_tn(x0_ref[e, :, part], grads[0][e // 2][span, :]) + mm_tn(
                x1_ref[e, :, part], grads[1][e // 2][span, :]
            )
            d_sel = mm(rows[0], x0_ref[e, :, part]) + mm(rows[1], x1_ref[e, :, part])
            sel_ref[pl.ds(at, 1), cols] = d_sel[e : e + 1, :]


def add_swapped_body(own_ref, got_ref, *outs):
    for g in range(GROUPS):
        span = slice(g * GTOK, (g + 1) * GTOK)
        outs[g][:, :] = (own_ref[span, :].astype(F32) + got_ref[span, :].astype(F32)).astype(BF)


def add_second_body(a, b, c, d, *outs):
    for i in range(4):
        span = slice(i * 256, (i + 1) * 256)
        outs[i][:, :] = sum(r[span, :].astype(F32) for r in (a, b, c, d)).astype(BF)


def gather_chip(mine, extra=None):
    pieces = [mine] + [hop(mine, 1, -d) for d in (1, 2, 3)]
    rows = 2 * TOK
    stacked = jnp.concatenate([q[:rows] for q in pieces] + [q[rows:] for q in pieces if q.shape[0] > rows], axis=0)
    own = [stacked] + [hop(stacked, 2, -d) for d in (1, 2, 3)]
    oth = [swap(q[:GTOK]) for q in own]
    return own, oth


def scatter_chip(own, oth):
    outs = [shape((GTOK, HALF), BF)] * 4
    second = call(add_swapped_body, outs, (own, swap(oth)), bytes_accessed=6 << 20)
    got = [second[0]] + [hop(second[d], 2, d) for d in (1, 2, 3)]
    first = call(add_second_body, [shape((2 * TOK, HALF), BF)] * 4, got, bytes_accessed=3 << 20)
    return [first[0]] + [hop(first[d], 1, d) for d in (1, 2, 3)]


def all_dp(block):
    return [block] + [hop_dp(block, -d) for d in (1, 2, 3)]


def to_dp(parts):
    return [parts[0]] + [hop_dp(parts[d], d) for d in (1, 2, 3)]


def per_device(tokens, picks, halting, w_sel, w_up, w_down, cotangent):
    dp = lax.axis_index("dp")
    place = lax.axis_index("expert")
    core = lax.rem(place, 2)
    sc = jnp.stack([dp, core]).astype(jnp.int32)
    rel = lax.rem(2 * dp + jnp.arange(NE, dtype=jnp.int32), NE) + NE * place
    eid = jnp.broadcast_to(rel.astype(F32)[:, None], (NE, 256))
    sel = w_sel.T[rel]
    sel = jnp.where(core == 0, sel, jnp.concatenate([sel[:, HALF:], sel[:, :HALF]], axis=1))

    def mine_of(array):
        return jnp.where(core == 0, array[:, :HALF], array[:, HALF:])

    def rest_of(array):
        return jnp.where(core == 0, array[:, HALF:], array[:, :HALF])

    live = halting[None, :, None] > jnp.arange(2, dtype=jnp.int32)[:, None, None]
    named = jnp.where(live, picks, 256).transpose(2, 0, 1).reshape(16, 256).astype(BF)
    rest = swap(jnp.concatenate([rest_of(tokens), named], axis=0))
    state = jnp.concatenate([mine_of(tokens), rest[:TOK]], axis=0)
    cot = jnp.concatenate([mine_of(cotangent), swap(rest_of(cotangent))], axis=0)

    own, oth = gather_chip(jnp.concatenate([state, named, rest[TOK:]], axis=0))
    v, vt = call(
        routing_body,
        [shape((2, GROUPS, NE, GTOK), F32), shape((2, GROUPS, GTOK, TOK), BF)],
        (eid, *own),
        bytes_accessed=6 << 20,
    )

    rows_type = shape((NE, ESLOT, 2 * HALF), BF)
    gather_flops = 2 * 640 * 1024 * 512 * 4 + 2 * 2560 * 512 * 256

    def project_up(p, own, oth):
        outs = [rows_type] + [shape((OWN + EXT, HID), BF)] * 4
        return call(
            up_body, outs, (sc, v[p], w_up, sel, *own, *oth), flops=gather_flops, bytes_accessed=12 << 20, smem=1
        )

    def project_cot(p, own, oth):
        outs = [rows_type] + [shape((OWN, HID), BF)] * 4
        return call(
            down_grad_body, outs, (sc, v[p], w_down, *own, *oth), flops=gather_flops, bytes_accessed=12 << 20, smem=1
        )

    def settle(parts):
        outs = [shape((OWN, HID), BF), shape((OWN, HID), F32), shape((OWN, TOK), F32)]
        return call(settle_body, outs, to_dp(parts), bytes_accessed=3 << 20)

    def settle_grad(parts, pre, gate):
        return call(settle_grad_body, shape((OWN + EXT, HID), BF), (*parts, pre, gate), bytes_accessed=3 << 20)

    spread = [shape((GROUPS * GTOK, HALF), BF)] * 2
    out_scratch = [pltpu.VMEM((GROUPS, NE * GSLOT, 2 * HALF), BF)]

    def outputs(p, hid):
        return call(
            down_body,
            spread,
            (sc, vt[p], w_down, *hid),
            flops=gather_flops,
            bytes_accessed=10 << 20,
            scratch=out_scratch,
            smem=1,
        )

    def grads_in(p, grads):
        return call(
            up_grad_body,
            spread,
            (sc, vt[p], w_up, sel, *grads),
            flops=gather_flops,
            bytes_accessed=10 << 20,
            scratch=out_scratch,
            smem=1,
        )

    def advance(base, terms):
        return (base.astype(F32) + sum(t.astype(F32) for t in terms)).astype(BF)

    x0, *parts = project_up(0, own, oth)
    hid0, pre0, gate0 = settle(parts)
    c1, *cot_parts = project_cot(1, *gather_chip(cot))
    cot_parts = to_dp(cot_parts)
    hid0 = all_dp(hid0)
    state1 = advance(state, scatter_chip(*outputs(0, hid0)))

    own, oth = gather_chip(state1)
    x1, *parts = project_up(1, own, oth)
    hid1, pre1, gate1 = settle(parts)
    grad1 = all_dp(settle_grad(cot_parts, pre1, gate1))
    hid1 = all_dp(hid1)

    cot1 = advance(cot, scatter_chip(*grads_in(1, grad1)))
    state2 = advance(state1, scatter_chip(*outputs(1, hid1)))

    c0, *cot_parts = project_cot(0, *gather_chip(cot1))
    grad0 = all_dp(settle_grad(to_dp(cot_parts), pre0, gate0))
    d_down = call(
        d_down_body,
        shape(w_down.shape, F32),
        (sc, c0, c1, *hid0, *hid1),
        flops=4 * 2560 * 512 * 256,
        bytes_accessed=16 << 20,
        smem=1,
    )
    cot0 = advance(cot1, scatter_chip(*grads_in(0, grad0)))
    d_up, d_sel = call(
        d_up_body,
        [shape(w_up.shape, F32), shape((NE, 2 * HALF), F32)],
        (sc, x0, x1, *grad0, *grad1),
        flops=4 * 2560 * 512 * 256,
        bytes_accessed=16 << 20,
        smem=1,
    )
    d_sel = lax.all_gather(d_sel, "expert", axis=0, tiled=True).T

    def whole(array):
        mine, rest = array[:TOK], swap(array[TOK:])
        return jnp.where(
            core == 0, jnp.concatenate([mine, rest], axis=1), jnp.concatenate([rest, mine], axis=1)
        )

    return (whole(state2), whole(cot0), d_up, d_down, d_sel)


def solution(mesh):
    in_specs = (
        P("expert", "dp"),
        P(None, "expert", None),
        P("expert"),
        P("dp", None),
        P("expert", "dp", None),
        P("expert", None, "dp"),
        P("expert", "dp"),
    )
    out_specs = (
        P("expert", "dp"),
        P("expert", "dp"),
        P("expert", "dp", None),
        P("expert", None, "dp"),
        P("dp", None),
    )
    return jax.shard_map(
        per_device, mesh=mesh, in_specs=in_specs, out_specs=out_specs, check_vma=False
    )
```

time: 1020 us -> 520 us (0.51)
  local copies, waits for them, and re-layouts: 300 us -> 27 us
  blocking collectives: 222 us -> 24.9 us
  waiting for transfers between devices: 338 us -> 191 us
  Pallas kernels: 0 us -> 129 us
  starting transfers between devices: 42.4 us -> 131 us
  matrix products: 48.4 us -> 0 us
  other arithmetic: 49.9 us -> 7.18 us
  between operations: 14.8 us -> 1.78 us
    psum x5 -> x0, waiting for transfers between devices: 240 us -> none  [the longest x4 140 us: settle(): lax.psum(partials.astype(jnp.bfloat16), 'dp').astype(jnp.float32)]
    ppermute x0 -> x96, waiting for transfers between devices: none -> 191 us  [the longest x48 96.2 us: hop(): return lax.ppermute(value, 'expert', along(axis, step % 4))]
    gather x22 -> x1, local copies, waits for them, and re-layouts: 189 us -> 0.57 us  [per_device(): sel = w_sel.T[rel]]
    all_to_all x3 -> x0, blocking collectives: 181 us -> none  [to_experts(): lax.all_to_all(buffer.reshape(experts, capacity, width_part), 'expert', s...]
    ppermute x0 -> x96, starting transfers between devices: none -> 131 us  [the longest x24 58.4 us: swap(): return lax.ppermute(value, 'expert', SWAP)]
    pallas_call x0 -> x23, Pallas kernels: none -> 129 us  [call(): pl.pallas_call(body, out_shape=outs, in_specs=[SMEM] * smem + [VMEM] * (l...]
    all_to_all x5 -> x0, waiting for transfers between devices: 97.3 us -> none  [the longest x4 49.7 us: to_tokens(): lax.all_to_all(buffer, 'expert', split_axis=1, concat_axis=0, tiled=True)]
    dot_general x18 -> x0, matrix products: 48.4 us -> none  [the longest x2 13.5 us: per_device(): jnp.einsum('erd,erh->edh', received, grad_pre, preferred_element_type=jnp...]
  transfers between devices with their start and end apart: 10 -> 96, of which waited for: 8 -> 46; matrix products, arithmetic and copies ran while one was open for 12% -> 2% of each run, Pallas kernels for 0% -> 16%
where the time goes in v1:
time: 520 us; the launch traced here: 512 us
  waiting for transfers between devices  191 us (37%)
  starting transfers between devices  131 us (25%)
  Pallas kernels  129 us (25%)
  local copies, waits for them, and re-layouts  27 us (5%)
  blocking collectives  24.9 us (5%)
  other arithmetic  7.18 us (1%)
    pallas_call x23, Pallas kernels, call(): pl.pallas_call(body, out_shape=outs, in_specs=[SMEM] * smem + [VMEM] * (l...  129 us
    ppermute x48, waiting for transfers between devices, hop(): return lax.ppermute(value, 'expert', along(axis, step % 4))  96.2 us
    ppermute x24, waiting for transfers between devices, hop_dp(): return lax.ppermute(value, 'dp', [(y, (y + step) % 4) for y in range(4)])  84 us
    ppermute x24, starting transfers between devices, swap(): return lax.ppermute(value, 'expert', SWAP)  58.4 us
    ppermute x48, starting transfers between devices, hop(): return lax.ppermute(value, 'expert', along(axis, step % 4))  46.8 us
    ppermute x24, starting transfers between devices, hop_dp(): return lax.ppermute(value, 'dp', [(y, (y + step) % 4) for y in range(4)])  25.7 us
    all_gather x1, blocking collectives, per_device(): d_sel = lax.all_gather(d_sel, 'expert', axis=0, tiled=True).T  24.9 us
    unnamed x170, local copies, waits for them, and re-layouts  22.4 us
  transfers between devices with their start and end apart: 96, of which 46 were waited for; matrix products, arithmetic and copies ran while one was open for 2% of the time, Pallas kernels for 16%

profile of v1, /device:TPU:1, one launch (start us, length us, event | category | flops | bytes accessed | tf_op | source)
XLA Modules:
  0.0 512.0 jit_solution(12336487316873586105)
XLA Ops:
  5.5 3.9 collective-permute-start.1
  23.3 8.7 %collective-permute-done.4.refs_1_ = bf16[1152,256]{1,0:T(8,128)(2,1)S(1)} collective-permute-done((bf16[1152,256]{1,0:T(8,128)(2,1)S(1)}, bf16[1152,256]{1,0:T(8,128)(2,1)S(1)}, u32[]{:S(2)}, u32[]{:S(2)}) %collective-permute-start.4) | collective-permute-done | bytes 589856 | tf_op jit(solution)/shard_map/ppermute | solution.py:48
  40.5 3.8 shard_map.110
  47.4 8.9 %shard_map.111 = (bf16[8,320,512]{2,1,0:T(8,128)(2,1)}, bf16[656,256]{1,0:T(8,128)(2,1)}, bf16[656,256]{1,0:T(8,128)(2,1)}, bf16[656,256]{1,0:T(8,128)(2,1)}, bf16[656,256]{1,0:T(8,128)(2,1)}) custom-call(s32[2]{0:T(128)} %pad_add_fusion.sc_ref, f32[4,8,1024]{2,1,0:T(8,128)} %get-tuple-element.156.v_ref, bf16[8,512,256]{2,1,0:T(8,128)(2,1)} %w_up_ref.7, ...), custom_call_target="tpu_custom_call" | custom-call | flops 3355443200 | bytes 12582912 | tf_op jit(solution)/shard_map/pallas_call | solution.py:60
  61.3 6.1 %collective-permute-done.11.p1 = bf16[656,256]{1,0:T(8,128)(2,1)S(1)} collective-permute-done((bf16[656,256]{1,0:T(8,128)(2,1)}, bf16[656,256]{1,0:T(8,128)(2,1)S(1)}, u32[]{:S(2)}, u32[]{:S(2)}) %collective-permute-start.11) | collective-permute-done | bytes 335904 | tf_op jit(solution)/shard_map/ppermute | solution.py:56
  67.4 8.3 %collective-permute-done.12.p2 = bf16[656,256]{1,0:T(8,128)(2,1)S(1)} collective-permute-done((bf16[656,256]{1,0:T(8,128)(2,1)}, bf16[656,256]{1,0:T(8,128)(2,1)S(1)}, u32[]{:S(2)}, u32[]{:S(2)}) %collective-permute-start.12) | collective-permute-done | bytes 335904 | tf_op jit(solution)/shard_map/ppermute | solution.py:56
  83.7 5.3 %collective-permute-done.14.h1.refs_1_ = bf16[640,256]{1,0:T(8,128)(2,1)S(1)} collective-permute-done((bf16[640,256]{1,0:T(8,128)(2,1)}, bf16[640,256]{1,0:T(8,128)(2,1)S(1)}, u32[]{:S(2)}, u32[]{:S(2)}) %collective-permute-start.14) | collective-permute-done | bytes 327712 | tf_op jit(solution)/shard_map/ppermute | solution.py:56
  91.6 8.1 %collective-permute-done.16.h3.refs_3_ = bf16[640,256]{1,0:T(8,128)(2,1)S(1)} collective-permute-done((bf16[640,256]{1,0:T(8,128)(2,1)}, bf16[640,256]{1,0:T(8,128)(2,1)S(1)}, u32[]{:S(2)}, u32[]{:S(2)}) %collective-permute-start.16) | collective-permute-done | bytes 327712 | tf_op jit(solution)/shard_map/ppermute | solution.py:56
  100.5 9.8 %shard_map.113 = (bf16[4096,256]{1,0:T(8,128)(2,1)}, bf16[4096,256]{1,0:T(8,128)(2,1)}) custom-call(s32[2]{0:T(128)} %pad_add_fusion.sc_ref, bf16[4,1024,128]{2,1,0:T(8,128)(2,1)} %get-tuple-element.154.vt_ref, bf16[8,256,512]{2,1,0:T(8,128)(2,1)} %w_down_ref.7, bf16[640,256]{1,0:T(8,128)(2,1)} %get-tuple-element.81.h0.refs_0_, bf16[640,256]{1,0:T(8,128)(2,1)} %copy-done.35, ...), custom_call_target="tpu_custom_call" | custom-call | flops 3355443200 | bytes 10485760 | tf_op jit(solution)/shard_map/pallas_call | solution.py:60
  110.8 4.0 collective-permute-done.17.got_ref
  116.1 3.7 shard_map.114
  127.2 9.3 %collective-permute-done.18.b = bf16[1024,256]{1,0:T(8,128)(2,1)S(1)} collective-permute-done((bf16[1024,256]{1,0:T(8,128)(2,1)}, bf16[1024,256]{1,0:T(8,128)(2,1)S(1)}, u32[]{:S(2)}, u32[]{:S(2)}) %collective-permute-start.18) | collective-permute-done | bytes 524320 | tf_op jit(solution)/shard_map/ppermute | solution.py:48
  160.9 9.3 %collective-permute-done.52.refs_1_ = bf16[1024,256]{1,0:T(8,128)(2,1)S(1)} collective-permute-done((bf16[1024,256]{1,0:T(8,128)(2,1)S(1)}, bf16[1024,256]{1,0:T(8,128)(2,1)S(1)}, u32[]{:S(2)}, u32[]{:S(2)}) %collective-permute-start.52) | collective-permute-done | bytes 524320 | tf_op jit(solution)/shard_map/ppermute | solution.py:48
  170.2 8.3 %collective-permute-start.30 = (bf16[1024,256]{1,0:T(8,128)(2,1)S(1)}, bf16[1024,256]{1,0:T(8,128)(2,1)S(1)}, u32[]{:S(2)}, u32[]{:S(2)}) collective-permute-start(bf16[1024,256]{1,0:T(8,128)(2,1)S(1)} %pad_maximum_fusion.refs_0_), channel_id=1, source_target_pairs={{0,1},{1,0},{2,3},{3,2},{4,5},{5,4},{6,7},{7,6},{8,9},{9,8},{10,11... | collective-permute-start | bytes 1572872 | tf_op jit(solution)/shard_map/ppermute | solution.py:52
  181.4 5.7 %collective-permute-start.31 = (bf16[1024,256]{1,0:T(8,128)(2,1)S(1)}, bf16[1024,256]{1,0:T(8,128)(2,1)S(1)}, u32[]{:S(2)}, u32[]{:S(2)}) collective-permute-start(bf16[1024,256]{1,0:T(8,128)(2,1)S(1)} %collective-permute-done.27.refs_1_), channel_id=1, source_target_pairs={{0,1},{1,0},{2,3},{3,2},{4,5},{5,4},{6,7},{7,6},{8,9},{9,8},{10,11... | collective-permute-start | bytes 1572872 | tf_op jit(solution)/shard_map/ppermute | solution.py:52
  187.2 3.8 collective-permute-start.33
  191.0 5.6 %collective-permute-start.55 = (bf16[1024,256]{1,0:T(8,128)(2,1)S(1)}, bf16[1024,256]{1,0:T(8,128)(2,1)S(1)}, u32[]{:S(2)}, u32[]{:S(2)}) collective-permute-start(bf16[1024,256]{1,0:T(8,128)(2,1)S(1)} %constant_dynamic-update-slice_fusion.9.refs_0_), channel_id=1, source_target_pairs={{0,1},{1,0},{2,3},{3,2},{4,5},{5,4},{6,7},{7,6},{8,9},{9,8},{10,11... | collective-permute-start | bytes 1572872 | tf_op jit(solution)/shard_map/ppermute | solution.py:52
  198.8 8.7 %shard_map.116 = (bf16[8,320,512]{2,1,0:T(8,128)(2,1)}, bf16[656,256]{1,0:T(8,128)(2,1)}, bf16[656,256]{1,0:T(8,128)(2,1)}, bf16[656,256]{1,0:T(8,128)(2,1)}, bf16[656,256]{1,0:T(8,128)(2,1)}) custom-call(s32[2]{0:T(128)} %pad_add_fusion.sc_ref, f32[4,8,1024]{2,1,0:T(8,128)} %get-tuple-element.157.v_ref, bf16[8,512,256]{2,1,0:T(8,128)(2,1)} %w_up_ref.7, ...), custom_call_target="tpu_custom_call" | custom-call | flops 3355443200 | bytes 12582912 | tf_op jit(solution)/shard_map/pallas_call | solution.py:60
  212.0 7.8 %shard_map.121 = (bf16[8,320,512]{2,1,0:T(8,128)(2,1)}, bf16[640,256]{1,0:T(8,128)(2,1)}, bf16[640,256]{1,0:T(8,128)(2,1)}, bf16[640,256]{1,0:T(8,128)(2,1)}, bf16[640,256]{1,0:T(8,128)(2,1)}) custom-call(s32[2]{0:T(128)} %pad_add_fusion.sc_ref, f32[4,8,1024]{2,1,0:T(8,128)} %get-tuple-element.157.v_ref, bf16[8,256,512]{2,1,0:T(8,128)(2,1)} %w_down_ref.7, ...), custom_call_target="tpu_custom_call" | custom-call | flops 3355443200 | bytes 12582912 | tf_op jit(solution)/shard_map/pallas_call | solution.py:60
  222.2 3.4 collective-permute-done.34.p1
  229.6 10.0 %collective-permute-done.59.p1 = bf16[640,256]{1,0:T(8,128)(2,1)S(1)} collective-permute-done((bf16[640,256]{1,0:T(8,128)(2,1)}, bf16[640,256]{1,0:T(8,128)(2,1)S(1)}, u32[]{:S(2)}, u32[]{:S(2)}) %collective-permute-start.59) | collective-permute-done | bytes 327712 | tf_op jit(solution)/shard_map/ppermute | solution.py:56
  240.7 3.1 shard_map.122.h0.refs_4_
  247.5 13.6 %collective-permute-done.62.h1.refs_5_ = bf16[656,256]{1,0:T(8,128)(2,1)S(1)} collective-permute-done((bf16[656,256]{1,0:T(8,128)(2,1)}, bf16[656,256]{1,0:T(8,128)(2,1)S(1)}, u32[]{:S(2)}, u32[]{:S(2)}) %collective-permute-start.62) | collective-permute-done | bytes 335904 | tf_op jit(solution)/shard_map/ppermute | solution.py:56
  261.1 4.0 collective-permute-done.64.h3.refs_7_
  265.8 10.0 %shard_map.123 = (bf16[4096,256]{1,0:T(8,128)(2,1)}, bf16[4096,256]{1,0:T(8,128)(2,1)}) custom-call(s32[2]{0:T(128)} %pad_add_fusion.sc_ref, bf16[4,1024,128]{2,1,0:T(8,128)(2,1)} %get-tuple-element.155.vt_ref, bf16[8,512,256]{2,1,0:T(8,128)(2,1)} %w_up_ref.7, bf16[8,512]{1,0:T(8,128)(2,1)} %maximum_select_fusion.2.sel_ref, ...), custom_call_target="tpu_custom_call" | custom-call | flops 3355443200 | bytes 10485760 | tf_op jit(solution)/shard_map/pallas_call | solution.py:60
  276.7 4.0 collective-permute-done.65.got_ref
  282.0 3.7 shard_map.124
  288.4 12.7 %collective-permute-done.66.b = bf16[1024,256]{1,0:T(8,128)(2,1)S(1)} collective-permute-done((bf16[1024,256]{1,0:T(8,128)(2,1)}, bf16[1024,256]{1,0:T(8,128)(2,1)S(1)}, u32[]{:S(2)}, u32[]{:S(2)}) %collective-permute-start.66) | collective-permute-done | bytes 524320 | tf_op jit(solution)/shard_map/ppermute | solution.py:48
  316.3 4.0 collective-permute-done.74
  323.5 4.1 collective-permute-start.78
  327.6 6.8 %collective-permute-done.75.refs_1_ = bf16[1024,256]{1,0:T(8,128)(2,1)S(1)} collective-permute-done((bf16[1024,256]{1,0:T(8,128)(2,1)S(1)}, bf16[1024,256]{1,0:T(8,128)(2,1)S(1)}, u32[]{:S(2)}, u32[]{:S(2)}) %collective-permute-start.75) | collective-permute-done | bytes 524320 | tf_op jit(solution)/shard_map/ppermute | solution.py:48
  334.4 4.4 collective-permute-start.79
  338.9 3.8 collective-permute-start.81
  345.9 7.9 %shard_map.126 = (bf16[8,320,512]{2,1,0:T(8,128)(2,1)}, bf16[640,256]{1,0:T(8,128)(2,1)}, bf16[640,256]{1,0:T(8,128)(2,1)}, bf16[640,256]{1,0:T(8,128)(2,1)}, bf16[640,256]{1,0:T(8,128)(2,1)}) custom-call(s32[2]{0:T(128)} %pad_add_fusion.sc_ref, f32[4,8,1024]{2,1,0:T(8,128)} %get-tuple-element.156.v_ref, bf16[8,256,512]{2,1,0:T(8,128)(2,1)} %w_down_ref.7, ...), custom_call_target="tpu_custom_call" | custom-call | flops 3355443200 | bytes 12582912 | tf_op jit(solution)/shard_map/pallas_call | solution.py:60
  362.3 9.8 %shard_map.118 = (bf16[4096,256]{1,0:T(8,128)(2,1)}, bf16[4096,256]{1,0:T(8,128)(2,1)}) custom-call(s32[2]{0:T(128)} %pad_add_fusion.sc_ref, bf16[4,1024,128]{2,1,0:T(8,128)(2,1)} %get-tuple-element.155.vt_ref, bf16[8,256,512]{2,1,0:T(8,128)(2,1)} %w_down_ref.7, bf16[640,256]{1,0:T(8,128)(2,1)} %get-tuple-element.96.h0.refs_4_, bf16[640,256]{1,0:T(8,128)(2,1)} %copy-done.39, ...), custom_call_target="tpu_custom_call" | custom-call | flops 3355443200 | bytes 10485760 | tf_op jit(solution)/shard_map/pallas_call | solution.py:60
  380.4 6.9 %collective-permute-done.85.h1.refs_1_ = bf16[656,256]{1,0:T(8,128)(2,1)S(1)} collective-permute-done((bf16[656,256]{1,0:T(8,128)(2,1)}, bf16[656,256]{1,0:T(8,128)(2,1)S(1)}, u32[]{:S(2)}, u32[]{:S(2)}) %collective-permute-start.85) | collective-permute-done | bytes 335904 | tf_op jit(solution)/shard_map/ppermute | solution.py:56
  390.1 8.3 %collective-permute-done.87.h3.refs_3_ = bf16[656,256]{1,0:T(8,128)(2,1)S(1)} collective-permute-done((bf16[656,256]{1,0:T(8,128)(2,1)}, bf16[656,256]{1,0:T(8,128)(2,1)S(1)}, u32[]{:S(2)}, u32[]{:S(2)}) %collective-permute-start.87) | collective-permute-done | bytes 335904 | tf_op jit(solution)/shard_map/ppermute | solution.py:56
  399.2 10.1 %shard_map.128 = (bf16[4096,256]{1,0:T(8,128)(2,1)}, bf16[4096,256]{1,0:T(8,128)(2,1)}) custom-call(s32[2]{0:T(128)} %pad_add_fusion.sc_ref, bf16[4,1024,128]{2,1,0:T(8,128)(2,1)} %get-tuple-element.154.vt_ref, bf16[8,512,256]{2,1,0:T(8,128)(2,1)} %w_up_ref.7, bf16[8,512]{1,0:T(8,128)(2,1)} %maximum_select_fusion.2.sel_ref, ...), custom_call_target="tpu_custom_call" | custom-call | flops 3355443200 | bytes 10485760 | tf_op jit(solution)/shard_map/pallas_call | solution.py:60
  411.0 3.7 shard_map.119
  418.5 5.9 %collective-permute-done.41.b = bf16[1024,256]{1,0:T(8,128)(2,1)S(1)} collective-permute-done((bf16[1024,256]{1,0:T(8,128)(2,1)}, bf16[1024,256]{1,0:T(8,128)(2,1)S(1)}, u32[]{:S(2)}, u32[]{:S(2)}) %collective-permute-start.41) | collective-permute-done | bytes 524320 | tf_op jit(solution)/shard_map/ppermute | solution.py:48
  424.4 6.2 %collective-permute-done.42.c = bf16[1024,256]{1,0:T(8,128)(2,1)S(1)} collective-permute-done((bf16[1024,256]{1,0:T(8,128)(2,1)}, bf16[1024,256]{1,0:T(8,128)(2,1)S(1)}, u32[]{:S(2)}, u32[]{:S(2)}) %collective-permute-start.42) | collective-permute-done | bytes 524320 | tf_op jit(solution)/shard_map/ppermute | solution.py:48
  436.9 3.7 shard_map.129
  444.4 3.8 collective-permute-start.47
  451.1 5.6 %collective-permute-done.90.c = bf16[1024,256]{1,0:T(8,128)(2,1)S(1)} collective-permute-done((bf16[1024,256]{1,0:T(8,128)(2,1)}, bf16[1024,256]{1,0:T(8,128)(2,1)S(1)}, u32[]{:S(2)}, u32[]{:S(2)}) %collective-permute-start.90) | collective-permute-done | bytes 524320 | tf_op jit(solution)/shard_map/ppermute | solution.py:48
  464.2 7.6 %shard_map.132 = f32[8,256,512]{2,1,0:T(8,128)} custom-call(s32[2]{0:T(128)} %pad_add_fusion.sc_ref, bf16[8,320,512]{2,1,0:T(8,128)(2,1)} %get-tuple-element.142.c0_ref, bf16[8,320,512]{2,1,0:T(8,128)(2,1)} %get-tuple-element.143.c1_ref, bf16[640,256]{1,0:T(8,128)(2,1)} %get-tuple-element.81.h0.refs_0_, bf16[640,256]{1,0:T(8,128)(2,1)} %copy-done.35, ...), custom_call_target="tpu_custom_call" | custom-call | flops 1342177280 | bytes 16777216 | tf_op jit(solution)/shard_map/pallas_call | solution.py:60
  471.8 8.4 %shard_map.131 = (f32[8,512,256]{2,1,0:T(8,128)}, f32[8,512]{1,0:T(8,128)}) custom-call(s32[2]{0:T(128)} %pad_add_fusion.sc_ref, bf16[8,320,512]{2,1,0:T(8,128)(2,1)} %get-tuple-element.139.x0_ref, bf16[8,320,512]{2,1,0:T(8,128)(2,1)} %get-tuple-element.140.x1_ref, bf16[656,256]{1,0:T(8,128)(2,1)} %shard_map.127.h0.refs_0_, bf16[656,256]{1,0:T(8,128)(2,1)} %copy-done.32, ...), custom_call_target="tpu_custom_call" | custom-call | flops 1342177280 | bytes 16777216 | tf_op jit(solution)/shard_map/pallas_call | solution.py:60
  480.4 4.5 collective-permute-start.95
  484.9 24.9 %all_gather.3 = f32[256,512]{1,0:T(8,128)S(1)} all-gather(f32[8,512]{1,0:T(8,128)} %get-tuple-element.144), channel_id=1, replica_groups=mesh['dp'=4,'expert'=32] {'expert'}, dimensions={0}, use_global_device_ids=true | all-gather | bytes 540672 | tf_op jit(solution)/shard_map/all_gather | solution.py:465
  (373 shorter events, 176.2 us)
Async XLA Ops:
  16.6 15.4 %collective-permute-start.4 = (bf16[1152,256]{1,0:T(8,128)(2,1)S(1)}, bf16[1152,256]{1,0:T(8,128)(2,1)S(1)}, u32[]{:S(2)}, u32[]{:S(2)}) collective-permute-start(bf16[1152,256]{1,0:T(8,128)(2,1)S(1)} %constant_dynamic-update-slice_fusion.refs_0_), channel_id=1, source_target_pairs={{0,6},{1,25},{2,0},{3,27},{4,2},{5,29},{6,4},{7,31},{8,14},{9,1},{... | collective-permute-start | bytes 1769480 | tf_op jit(solution)/shard_map/ppermute | solution.py:48
  18.8 16.2 %collective-permute-start.5 = (bf16[1152,256]{1,0:T(8,128)(2,1)S(1)}, bf16[1152,256]{1,0:T(8,128)(2,1)S(1)}, u32[]{:S(2)}, u32[]{:S(2)}) collective-permute-start(bf16[1152,256]{1,0:T(8,128)(2,1)S(1)} %constant_dynamic-update-slice_fusion.refs_0_), channel_id=1, source_target_pairs={{0,4},{1,17},{2,6},{3,19},{4,0},{5,21},{6,2},{7,23},{8,12},{9,25},... | collective-permute-start | bytes 1769480 | tf_op jit(solution)/shard_map/ppermute | solution.py:48
  19.3 16.3 %collective-permute-start.6 = (bf16[1152,256]{1,0:T(8,128)(2,1)S(1)}, bf16[1152,256]{1,0:T(8,128)(2,1)S(1)}, u32[]{:S(2)}, u32[]{:S(2)}) collective-permute-start(bf16[1152,256]{1,0:T(8,128)(2,1)S(1)} %constant_dynamic-update-slice_fusion.refs_0_), channel_id=1, source_target_pairs={{0,2},{1,9},{2,4},{3,11},{4,6},{5,13},{6,0},{7,15},{8,10},{9,17},{... | collective-permute-start | bytes 1769480 | tf_op jit(solution)/shard_map/ppermute | solution.py:48
  20.7 25.3 %collective-permute-start.7 = (bf16[1024,256]{1,0:T(8,128)(2,1)S(1)}, bf16[1024,256]{1,0:T(8,128)(2,1)S(1)}, u32[]{:S(2)}, u32[]{:S(2)}) collective-permute-start(bf16[1024,256]{1,0:T(8,128)(2,1)S(1)} %get-tuple-element.158), channel_id=1, source_target_pairs={{0,1},{1,0},{2,3},{3,2},{4,5},{5,4},{6,7},{7,6},{8,9},{9,8},{10,11... | collective-permute-start | bytes 1572872 | tf_op jit(solution)/shard_map/ppermute | solution.py:52
  57.6 18.1 %collective-permute-start.12 = (bf16[656,256]{1,0:T(8,128)(2,1)}, bf16[656,256]{1,0:T(8,128)(2,1)S(1)}, u32[]{:S(2)}, u32[]{:S(2)}) collective-permute-start(bf16[656,256]{1,0:T(8,128)(2,1)} %get-tuple-element.79), channel_id=1, source_target_pairs={{0,64},{32,96},{64,0},{96,32},{1,65},{33,97},{65,1},{97,33},{2,66}... | collective-permute-start | bytes 1007624 | tf_op jit(solution)/shard_map/ppermute | solution.py:56
  60.3 15.5 %collective-permute-start.13 = (bf16[656,256]{1,0:T(8,128)(2,1)}, bf16[656,256]{1,0:T(8,128)(2,1)S(1)}, u32[]{:S(2)}, u32[]{:S(2)}) collective-permute-start(bf16[656,256]{1,0:T(8,128)(2,1)} %get-tuple-element.80), channel_id=1, source_target_pairs={{0,96},{32,0},{64,32},{96,64},{1,97},{33,1},{65,33},{97,65},{2,98}... | collective-permute-start | bytes 1007624 | tf_op jit(solution)/shard_map/ppermute | solution.py:56
  81.6 18.2 %collective-permute-start.16 = (bf16[640,256]{1,0:T(8,128)(2,1)}, bf16[640,256]{1,0:T(8,128)(2,1)S(1)}, u32[]{:S(2)}, u32[]{:S(2)}) collective-permute-start(bf16[640,256]{1,0:T(8,128)(2,1)} %get-tuple-element.81.h0.refs_0_), channel_id=1, source_target_pairs={{0,32},{32,64},{64,96},{96,0},{1,33},{33,65},{65,97},{97,1},{2,34}... | collective-permute-start | bytes 983048 | tf_op jit(solution)/shard_map/ppermute | solution.py:56
  119.8 16.8 %collective-permute-start.18 = (bf16[1024,256]{1,0:T(8,128)(2,1)}, bf16[1024,256]{1,0:T(8,128)(2,1)S(1)}, u32[]{:S(2)}, u32[]{:S(2)}) collective-permute-start(bf16[1024,256]{1,0:T(8,128)(2,1)} %get-tuple-element.85), channel_id=1, source_target_pairs={{0,2},{1,9},{2,4},{3,11},{4,6},{5,13},{6,0},{7,15},{8,10},{9,17},{... | collective-permute-start | bytes 1572872 | tf_op jit(solution)/shard_map/ppermute | solution.py:48
  119.8 16.8 %collective-permute-start.19 = (bf16[1024,256]{1,0:T(8,128)(2,1)}, bf16[1024,256]{1,0:T(8,128)(2,1)S(1)}, u32[]{:S(2)}, u32[]{:S(2)}) collective-permute-start(bf16[1024,256]{1,0:T(8,128)(2,1)} %get-tuple-element.86), channel_id=1, source_target_pairs={{0,4},{1,17},{2,6},{3,19},{4,0},{5,21},{6,2},{7,23},{8,12},{9,25},... | collective-permute-start | bytes 1572872 | tf_op jit(solution)/shard_map/ppermute | solution.py:48
  121.3 17.3 %collective-permute-start.20 = (bf16[1024,256]{1,0:T(8,128)(2,1)}, bf16[1024,256]{1,0:T(8,128)(2,1)S(1)}, u32[]{:S(2)}, u32[]{:S(2)}) collective-permute-start(bf16[1024,256]{1,0:T(8,128)(2,1)} %get-tuple-element.87), channel_id=1, source_target_pairs={{0,6},{1,25},{2,0},{3,27},{4,2},{5,29},{6,4},{7,31},{8,14},{9,1},{... | collective-permute-start | bytes 1572872 | tf_op jit(solution)/shard_map/ppermute | solution.py:48
  124.4 18.9 %collective-permute-start.49 = (bf16[256,256]{1,0:T(8,128)(2,1)S(1)}, bf16[256,256]{1,0:T(8,128)(2,1)S(1)}, u32[]{:S(2)}, u32[]{:S(2)}) collective-permute-start(bf16[256,256]{1,0:T(8,128)(2,1)S(1)} %pad_maximum_fusion.3), channel_id=1, source_target_pairs={{0,24},{1,7},{2,26},{3,1},{4,28},{5,3},{6,30},{7,5},{8,0},{9,15},{... | collective-permute-start | bytes 393224 | tf_op jit(solution)/shard_map/ppermute | solution.py:48
  125.1 28.4 %collective-permute-start.50 = (bf16[256,256]{1,0:T(8,128)(2,1)S(1)}, bf16[256,256]{1,0:T(8,128)(2,1)S(1)}, u32[]{:S(2)}, u32[]{:S(2)}) collective-permute-start(bf16[256,256]{1,0:T(8,128)(2,1)S(1)} %pad_maximum_fusion.3), channel_id=1, source_target_pairs={{0,16},{1,5},{2,18},{3,7},{4,20},{5,1},{6,22},{7,3},{8,24},{9,13},... | collective-permute-start | bytes 393224 | tf_op jit(solution)/shard_map/ppermute | solution.py:48
  153.5 16.7 %collective-permute-start.52 = (bf16[1024,256]{1,0:T(8,128)(2,1)S(1)}, bf16[1024,256]{1,0:T(8,128)(2,1)S(1)}, u32[]{:S(2)}, u32[]{:S(2)}) collective-permute-start(bf16[1024,256]{1,0:T(8,128)(2,1)S(1)} %constant_dynamic-update-slice_fusion.9.refs_0_), channel_id=1, source_target_pairs={{0,6},{1,25},{2,0},{3,27},{4,2},{5,29},{6,4},{7,31},{8,14},{9,1},{... | collective-permute-start | bytes 1572872 | tf_op jit(solution)/shard_map/ppermute | solution.py:48
  155.6 14.6 %collective-permute-start.53 = (bf16[1024,256]{1,0:T(8,128)(2,1)S(1)}, bf16[1024,256]{1,0:T(8,128)(2,1)S(1)}, u32[]{:S(2)}, u32[]{:S(2)}) collective-permute-start(bf16[1024,256]{1,0:T(8,128)(2,1)S(1)} %constant_dynamic-update-slice_fusion.9.refs_0_), channel_id=1, source_target_pairs={{0,4},{1,17},{2,6},{3,19},{4,0},{5,21},{6,2},{7,23},{8,12},{9,25},... | collective-permute-start | bytes 1572872 | tf_op jit(solution)/shard_map/ppermute | solution.py:48
  158.2 23.2 %collective-permute-start.27 = (bf16[1024,256]{1,0:T(8,128)(2,1)S(1)}, bf16[1024,256]{1,0:T(8,128)(2,1)S(1)}, u32[]{:S(2)}, u32[]{:S(2)}) collective-permute-start(bf16[1024,256]{1,0:T(8,128)(2,1)S(1)} %pad_maximum_fusion.refs_0_), channel_id=1, source_target_pairs={{0,6},{1,25},{2,0},{3,27},{4,2},{5,29},{6,4},{7,31},{8,14},{9,1},{... | collective-permute-start | bytes 1572872 | tf_op jit(solution)/shard_map/ppermute | solution.py:48
  160.0 27.1 %collective-permute-start.28 = (bf16[1024,256]{1,0:T(8,128)(2,1)S(1)}, bf16[1024,256]{1,0:T(8,128)(2,1)S(1)}, u32[]{:S(2)}, u32[]{:S(2)}) collective-permute-start(bf16[1024,256]{1,0:T(8,128)(2,1)S(1)} %pad_maximum_fusion.refs_0_), channel_id=1, source_target_pairs={{0,4},{1,17},{2,6},{3,19},{4,0},{5,21},{6,2},{7,23},{8,12},{9,25},... | collective-permute-start | bytes 1572872 | tf_op jit(solution)/shard_map/ppermute | solution.py:48
  160.0 27.2 %collective-permute-start.29 = (bf16[1024,256]{1,0:T(8,128)(2,1)S(1)}, bf16[1024,256]{1,0:T(8,128)(2,1)S(1)}, u32[]{:S(2)}, u32[]{:S(2)}) collective-permute-start(bf16[1024,256]{1,0:T(8,128)(2,1)S(1)} %pad_maximum_fusion.refs_0_), channel_id=1, source_target_pairs={{0,2},{1,9},{2,4},{3,11},{4,6},{5,13},{6,0},{7,15},{8,10},{9,17},{... | collective-permute-start | bytes 1572872 | tf_op jit(solution)/shard_map/ppermute | solution.py:48
  170.2 20.8 %collective-permute-start.54 = (bf16[1024,256]{1,0:T(8,128)(2,1)S(1)}, bf16[1024,256]{1,0:T(8,128)(2,1)S(1)}, u32[]{:S(2)}, u32[]{:S(2)}) collective-permute-start(bf16[1024,256]{1,0:T(8,128)(2,1)S(1)} %constant_dynamic-update-slice_fusion.9.refs_0_), channel_id=1, source_target_pairs={{0,2},{1,9},{2,4},{3,11},{4,6},{5,13},{6,0},{7,15},{8,10},{9,17},{... | collective-permute-start | bytes 1572872 | tf_op jit(solution)/shard_map/ppermute | solution.py:48
  170.2 26.4 %collective-permute-start.30 = (bf16[1024,256]{1,0:T(8,128)(2,1)S(1)}, bf16[1024,256]{1,0:T(8,128)(2,1)S(1)}, u32[]{:S(2)}, u32[]{:S(2)}) collective-permute-start(bf16[1024,256]{1,0:T(8,128)(2,1)S(1)} %pad_maximum_fusion.refs_0_), channel_id=1, source_target_pairs={{0,1},{1,0},{2,3},{3,2},{4,5},{5,4},{6,7},{7,6},{8,9},{9,8},{10,11... | collective-permute-start | bytes 1572872 | tf_op jit(solution)/shard_map/ppermute | solution.py:52
  181.4 15.3 %collective-permute-start.31 = (bf16[1024,256]{1,0:T(8,128)(2,1)S(1)}, bf16[1024,256]{1,0:T(8,128)(2,1)S(1)}, u32[]{:S(2)}, u32[]{:S(2)}) collective-permute-start(bf16[1024,256]{1,0:T(8,128)(2,1)S(1)} %collective-permute-done.27.refs_1_), channel_id=1, source_target_pairs={{0,1},{1,0},{2,3},{3,2},{4,5},{5,4},{6,7},{7,6},{8,9},{9,8},{10,11... | collective-permute-start | bytes 1572872 | tf_op jit(solution)/shard_map/ppermute | solution.py:52
  191.0 16.6 %collective-permute-start.55 = (bf16[1024,256]{1,0:T(8,128)(2,1)S(1)}, bf16[1024,256]{1,0:T(8,128)(2,1)S(1)}, u32[]{:S(2)}, u32[]{:S(2)}) collective-permute-start(bf16[1024,256]{1,0:T(8,128)(2,1)S(1)} %constant_dynamic-update-slice_fusion.9.refs_0_), channel_id=1, source_target_pairs={{0,1},{1,0},{2,3},{3,2},{4,5},{5,4},{6,7},{7,6},{8,9},{9,8},{10,11... | collective-permute-start | bytes 1572872 | tf_op jit(solution)/shard_map/ppermute | solution.py:52
  207.5 18.0 %collective-permute-start.34 = (bf16[656,256]{1,0:T(8,128)(2,1)}, bf16[656,256]{1,0:T(8,128)(2,1)S(1)}, u32[]{:S(2)}, u32[]{:S(2)}) collective-permute-start(bf16[656,256]{1,0:T(8,128)(2,1)} %get-tuple-element.93), channel_id=1, source_target_pairs={{0,32},{32,64},{64,96},{96,0},{1,33},{33,65},{65,97},{97,1},{2,34}... | collective-permute-start | bytes 1007624 | tf_op jit(solution)/shard_map/ppermute | solution.py:56
  207.6 18.3 %collective-permute-start.35 = (bf16[656,256]{1,0:T(8,128)(2,1)}, bf16[656,256]{1,0:T(8,128)(2,1)S(1)}, u32[]{:S(2)}, u32[]{:S(2)}) collective-permute-start(bf16[656,256]{1,0:T(8,128)(2,1)} %get-tuple-element.94), channel_id=1, source_target_pairs={{0,64},{32,96},{64,0},{96,32},{1,65},{33,97},{65,1},{97,33},{2,66}... | collective-permute-start | bytes 1007624 | tf_op jit(solution)/shard_map/ppermute | solution.py:56
  209.1 16.8 %collective-permute-start.36 = (bf16[656,256]{1,0:T(8,128)(2,1)}, bf16[656,256]{1,0:T(8,128)(2,1)S(1)}, u32[]{:S(2)}, u32[]{:S(2)}) collective-permute-start(bf16[656,256]{1,0:T(8,128)(2,1)} %get-tuple-element.95), channel_id=1, source_target_pairs={{0,96},{32,0},{64,32},{96,64},{1,97},{33,1},{65,33},{97,65},{2,98}... | collective-permute-start | bytes 1007624 | tf_op jit(solution)/shard_map/ppermute | solution.py:56
  219.8 19.8 %collective-permute-start.59 = (bf16[640,256]{1,0:T(8,128)(2,1)}, bf16[640,256]{1,0:T(8,128)(2,1)S(1)}, u32[]{:S(2)}, u32[]{:S(2)}) collective-permute-start(bf16[640,256]{1,0:T(8,128)(2,1)} %get-tuple-element.108), channel_id=1, source_target_pairs={{0,32},{32,64},{64,96},{96,0},{1,33},{33,65},{65,97},{97,1},{2,34}... | collective-permute-start | bytes 983048 | tf_op jit(solution)/shard_map/ppermute | solution.py:56
  220.5 19.1 %collective-permute-start.60 = (bf16[640,256]{1,0:T(8,128)(2,1)}, bf16[640,256]{1,0:T(8,128)(2,1)S(1)}, u32[]{:S(2)}, u32[]{:S(2)}) collective-permute-start(bf16[640,256]{1,0:T(8,128)(2,1)} %get-tuple-element.109), channel_id=1, source_target_pairs={{0,64},{32,96},{64,0},{96,32},{1,65},{33,97},{65,1},{97,33},{2,66}... | collective-permute-start | bytes 983048 | tf_op jit(solution)/shard_map/ppermute | solution.py:56
  243.8 17.3 %collective-permute-start.62 = (bf16[656,256]{1,0:T(8,128)(2,1)}, bf16[656,256]{1,0:T(8,128)(2,1)S(1)}, u32[]{:S(2)}, u32[]{:S(2)}) collective-permute-start(bf16[656,256]{1,0:T(8,128)(2,1)} %shard_map.122.h0.refs_4_), channel_id=1, source_target_pairs={{0,96},{32,0},{64,32},{96,64},{1,97},{33,1},{65,33},{97,65},{2,98}... | collective-permute-start | bytes 1007624 | tf_op jit(solution)/shard_map/ppermute | solution.py:56
  247.0 18.1 %collective-permute-start.64 = (bf16[656,256]{1,0:T(8,128)(2,1)}, bf16[656,256]{1,0:T(8,128)(2,1)S(1)}, u32[]{:S(2)}, u32[]{:S(2)}) collective-permute-start(bf16[656,256]{1,0:T(8,128)(2,1)} %shard_map.122.h0.refs_4_), channel_id=1, source_target_pairs={{0,32},{32,64},{64,96},{96,0},{1,33},{33,65},{65,97},{97,1},{2,34}... | collective-permute-start | bytes 1007624 | tf_op jit(solution)/shard_map/ppermute | solution.py:56
  285.7 15.4 %collective-permute-start.66 = (bf16[1024,256]{1,0:T(8,128)(2,1)}, bf16[1024,256]{1,0:T(8,128)(2,1)S(1)}, u32[]{:S(2)}, u32[]{:S(2)}) collective-permute-start(bf16[1024,256]{1,0:T(8,128)(2,1)} %get-tuple-element.116), channel_id=1, source_target_pairs={{0,2},{1,9},{2,4},{3,11},{4,6},{5,13},{6,0},{7,15},{8,10},{9,17},{... | collective-permute-start | bytes 1572872 | tf_op jit(solution)/shard_map/ppermute | solution.py:48
  285.7 15.4 %collective-permute-start.67 = (bf16[1024,256]{1,0:T(8,128)(2,1)}, bf16[1024,256]{1,0:T(8,128)(2,1)S(1)}, u32[]{:S(2)}, u32[]{:S(2)}) collective-permute-start(bf16[1024,256]{1,0:T(8,128)(2,1)} %get-tuple-element.117), channel_id=1, source_target_pairs={{0,4},{1,17},{2,6},{3,19},{4,0},{5,21},{6,2},{7,23},{8,12},{9,25},... | collective-permute-start | bytes 1572872 | tf_op jit(solution)/shard_map/ppermute | solution.py:48
  286.0 15.7 %collective-permute-start.68 = (bf16[1024,256]{1,0:T(8,128)(2,1)}, bf16[1024,256]{1,0:T(8,128)(2,1)S(1)}, u32[]{:S(2)}, u32[]{:S(2)}) collective-permute-start(bf16[1024,256]{1,0:T(8,128)(2,1)} %get-tuple-element.118), channel_id=1, source_target_pairs={{0,6},{1,25},{2,0},{3,27},{4,2},{5,29},{6,4},{7,31},{8,14},{9,1},{... | collective-permute-start | bytes 1572872 | tf_op jit(solution)/shard_map/ppermute | solution.py:48
  322.7 16.2 %collective-permute-start.76 = (bf16[1024,256]{1,0:T(8,128)(2,1)S(1)}, bf16[1024,256]{1,0:T(8,128)(2,1)S(1)}, u32[]{:S(2)}, u32[]{:S(2)}) collective-permute-start(bf16[1024,256]{1,0:T(8,128)(2,1)S(1)} %pad_maximum_fusion.1.refs_0_), channel_id=1, source_target_pairs={{0,4},{1,17},{2,6},{3,19},{4,0},{5,21},{6,2},{7,23},{8,12},{9,25},... | collective-permute-start | bytes 1572872 | tf_op jit(solution)/shard_map/ppermute | solution.py:48
  322.9 16.1 %collective-permute-start.77 = (bf16[1024,256]{1,0:T(8,128)(2,1)S(1)}, bf16[1024,256]{1,0:T(8,128)(2,1)S(1)}, u32[]{:S(2)}, u32[]{:S(2)}) collective-permute-start(bf16[1024,256]{1,0:T(8,128)(2,1)S(1)} %pad_maximum_fusion.1.refs_0_), channel_id=1, source_target_pairs={{0,2},{1,9},{2,4},{3,11},{4,6},{5,13},{6,0},{7,15},{8,10},{9,17},{... | collective-permute-start | bytes 1572872 | tf_op jit(solution)/shard_map/ppermute | solution.py:48
  323.5 19.8 %collective-permute-start.78 = (bf16[1024,256]{1,0:T(8,128)(2,1)S(1)}, bf16[1024,256]{1,0:T(8,128)(2,1)S(1)}, u32[]{:S(2)}, u32[]{:S(2)}) collective-permute-start(bf16[1024,256]{1,0:T(8,128)(2,1)S(1)} %pad_maximum_fusion.1.refs_0_), channel_id=1, source_target_pairs={{0,1},{1,0},{2,3},{3,2},{4,5},{5,4},{6,7},{7,6},{8,9},{9,8},{10,11... | collective-permute-start | bytes 1572872 | tf_op jit(solution)/shard_map/ppermute | solution.py:52
  342.7 14.7 %collective-permute-start.37 = (bf16[640,256]{1,0:T(8,128)(2,1)S(1)}, bf16[640,256]{1,0:T(8,128)(2,1)S(1)}, u32[]{:S(2)}, u32[]{:S(2)}) collective-permute-start(bf16[640,256]{1,0:T(8,128)(2,1)S(1)} %copy-done.38), channel_id=1, source_target_pairs={{0,96},{32,0},{64,32},{96,64},{1,97},{33,1},{65,33},{97,65},{2,98}... | collective-permute-start | bytes 983048 | tf_op jit(solution)/shard_map/ppermute | solution.py:56
  343.4 16.0 %collective-permute-start.38 = (bf16[640,256]{1,0:T(8,128)(2,1)S(1)}, bf16[640,256]{1,0:T(8,128)(2,1)S(1)}, u32[]{:S(2)}, u32[]{:S(2)}) collective-permute-start(bf16[640,256]{1,0:T(8,128)(2,1)S(1)} %copy-done.38), channel_id=1, source_target_pairs={{0,64},{32,96},{64,0},{96,32},{1,65},{33,97},{65,1},{97,33},{2,66}... | collective-permute-start | bytes 983048 | tf_op jit(solution)/shard_map/ppermute | solution.py:56
  343.4 18.1 %collective-permute-start.39 = (bf16[640,256]{1,0:T(8,128)(2,1)S(1)}, bf16[640,256]{1,0:T(8,128)(2,1)S(1)}, u32[]{:S(2)}, u32[]{:S(2)}) collective-permute-start(bf16[640,256]{1,0:T(8,128)(2,1)S(1)} %copy-done.38), channel_id=1, source_target_pairs={{0,32},{32,64},{64,96},{96,0},{1,33},{33,65},{65,97},{97,1},{2,34}... | collective-permute-start | bytes 983048 | tf_op jit(solution)/shard_map/ppermute | solution.py:56
  353.8 19.0 %collective-permute-start.82 = (bf16[640,256]{1,0:T(8,128)(2,1)}, bf16[640,256]{1,0:T(8,128)(2,1)S(1)}, u32[]{:S(2)}, u32[]{:S(2)}) collective-permute-start(bf16[640,256]{1,0:T(8,128)(2,1)} %get-tuple-element.124), channel_id=1, source_target_pairs={{0,32},{32,64},{64,96},{96,0},{1,33},{33,65},{65,97},{97,1},{2,34}... | collective-permute-start | bytes 983048 | tf_op jit(solution)/shard_map/ppermute | solution.py:56
  355.5 19.4 %collective-permute-start.83 = (bf16[640,256]{1,0:T(8,128)(2,1)}, bf16[640,256]{1,0:T(8,128)(2,1)S(1)}, u32[]{:S(2)}, u32[]{:S(2)}) collective-permute-start(bf16[640,256]{1,0:T(8,128)(2,1)} %get-tuple-element.125), channel_id=1, source_target_pairs={{0,64},{32,96},{64,0},{96,32},{1,65},{33,97},{65,1},{97,33},{2,66}... | collective-permute-start | bytes 983048 | tf_op jit(solution)/shard_map/ppermute | solution.py:56
  357.4 17.5 %collective-permute-start.84 = (bf16[640,256]{1,0:T(8,128)(2,1)}, bf16[640,256]{1,0:T(8,128)(2,1)S(1)}, u32[]{:S(2)}, u32[]{:S(2)}) collective-permute-start(bf16[640,256]{1,0:T(8,128)(2,1)} %get-tuple-element.126), channel_id=1, source_target_pairs={{0,96},{32,0},{64,32},{96,64},{1,97},{33,1},{65,33},{97,65},{2,98}... | collective-permute-start | bytes 983048 | tf_op jit(solution)/shard_map/ppermute | solution.py:56
  372.1 37.7 %collective-permute-start.40 = (bf16[4096,256]{1,0:T(8,128)(2,1)}, bf16[4096,256]{1,0:T(8,128)(2,1)S(1)}, u32[]{:S(2)}, u32[]{:S(2)}) collective-permute-start(bf16[4096,256]{1,0:T(8,128)(2,1)} %get-tuple-element.98), channel_id=1, source_target_pairs={{0,1},{1,0},{2,3},{3,2},{4,5},{5,4},{6,7},{7,6},{8,9},{9,8},{10,11... | collective-permute-start | bytes 6291464 | tf_op jit(solution)/shard_map/ppermute | solution.py:52
  379.7 18.7 %collective-permute-start.87 = (bf16[656,256]{1,0:T(8,128)(2,1)}, bf16[656,256]{1,0:T(8,128)(2,1)S(1)}, u32[]{:S(2)}, u32[]{:S(2)}) collective-permute-start(bf16[656,256]{1,0:T(8,128)(2,1)} %shard_map.127.h0.refs_0_), channel_id=1, source_target_pairs={{0,32},{32,64},{64,96},{96,0},{1,33},{33,65},{65,97},{97,1},{2,34}... | collective-permute-start | bytes 1007624 | tf_op jit(solution)/shard_map/ppermute | solution.py:56
  409.2 26.3 %collective-permute-start.88 = (bf16[4096,256]{1,0:T(8,128)(2,1)}, bf16[4096,256]{1,0:T(8,128)(2,1)S(1)}, u32[]{:S(2)}, u32[]{:S(2)}) collective-permute-start(bf16[4096,256]{1,0:T(8,128)(2,1)} %get-tuple-element.130), channel_id=1, source_target_pairs={{0,1},{1,0},{2,3},{3,2},{4,5},{5,4},{6,7},{7,6},{8,9},{9,8},{10,11... | collective-permute-start | bytes 6291464 | tf_op jit(solution)/shard_map/ppermute | solution.py:52
  441.5 15.1 %collective-permute-start.90 = (bf16[1024,256]{1,0:T(8,128)(2,1)}, bf16[1024,256]{1,0:T(8,128)(2,1)S(1)}, u32[]{:S(2)}, u32[]{:S(2)}) collective-permute-start(bf16[1024,256]{1,0:T(8,128)(2,1)} %get-tuple-element.133), channel_id=1, source_target_pairs={{0,4},{1,17},{2,6},{3,19},{4,0},{5,21},{6,2},{7,23},{8,12},{9,25},... | collective-permute-start | bytes 1572872 | tf_op jit(solution)/shard_map/ppermute | solution.py:48
  460.1 20.1 %collective-permute-start.94 = (bf16[256,256]{1,0:T(8,128)(2,1)}, bf16[256,256]{1,0:T(8,128)(2,1)S(1)}, u32[]{:S(2)}, u32[]{:S(2)}) collective-permute-start(bf16[256,256]{1,0:T(8,128)(2,1)} %get-tuple-element.138), channel_id=1, source_target_pairs={{0,24},{1,7},{2,26},{3,1},{4,28},{5,3},{6,30},{7,5},{8,0},{9,15},{... | collective-permute-start | bytes 393224 | tf_op jit(solution)/shard_map/ppermute | solution.py:48
  462.2 18.0 %collective-permute-start.93 = (bf16[256,256]{1,0:T(8,128)(2,1)}, bf16[256,256]{1,0:T(8,128)(2,1)S(1)}, u32[]{:S(2)}, u32[]{:S(2)}) collective-permute-start(bf16[256,256]{1,0:T(8,128)(2,1)} %get-tuple-element.137), channel_id=1, source_target_pairs={{0,16},{1,5},{2,18},{3,7},{4,20},{5,1},{6,22},{7,3},{8,24},{9,13},... | collective-permute-start | bytes 393224 | tf_op jit(solution)/shard_map/ppermute | solution.py:48
  463.4 16.8 %collective-permute-start.92 = (bf16[256,256]{1,0:T(8,128)(2,1)}, bf16[256,256]{1,0:T(8,128)(2,1)S(1)}, u32[]{:S(2)}, u32[]{:S(2)}) collective-permute-start(bf16[256,256]{1,0:T(8,128)(2,1)} %get-tuple-element.136), channel_id=1, source_target_pairs={{0,8},{1,3},{2,10},{3,5},{4,12},{5,7},{6,14},{7,1},{8,16},{9,11},{... | collective-permute-start | bytes 393224 | tf_op jit(solution)/shard_map/ppermute | solution.py:48
  480.4 30.5 %collective-permute-start.95 = (bf16[128,256]{1,0:T(8,128)(2,1)S(1)}, bf16[128,256]{1,0:T(8,128)(2,1)S(1)}, u32[]{:S(2)}, u32[]{:S(2)}) collective-permute-start(bf16[128,256]{1,0:T(8,128)(2,1)S(1)} %get-tuple-element.165), channel_id=1, source_target_pairs={{0,1},{1,0},{2,3},{3,2},{4,5},{5,4},{6,7},{7,6},{8,9},{9,8},{10,11... | collective-permute-start | bytes 196616 | tf_op jit(solution)/shard_map/ppermute | solution.py:52
  (127 other events, 1000.2 us)

commit v2 on v1

v2 whole, which is shorter than its diff:
```python
import functools

import jax
import jax.numpy as jnp
from jax import lax
from jax.experimental import pallas as pl
from jax.experimental.pallas import tpu as pltpu
from jax.sharding import PartitionSpec as P

BF = jnp.bfloat16
F32 = jnp.float32
GELU_C = 0.7978845608028654
GELU_A = 0.044715

TOK = 128
HALF = 256
HID = 256
NE = 8
CAP = 10
GRP = 8
GROUPS = 4
GTOK = GRP * TOK
GSLOT = GRP * CAP
ESLOT = GROUPS * GSLOT
OWN = 2 * ESLOT
EXT = 16
QUADS = 8
QTOK = 4 * TOK
QCAP = 4 * CAP
QSLOT = NE * QCAP
EXPERTS = 256
VMEM = pl.BlockSpec(memory_space=pltpu.VMEM)
HBM = pl.BlockSpec(memory_space=pl.ANY)
SMEM = pl.BlockSpec(memory_space=pltpu.SMEM)


def dev(x, z, c):
    return (x * 4 + z) * 2 + c


PLACES = [(x, z, c) for x in range(4) for z in range(4) for c in range(2)]
SWAP = [(dev(x, z, c), dev(x, z, 1 - c)) for x, z, c in PLACES]


def along(axis, step):
    pairs = []
    for x, z, c in PLACES:
        if (axis + c) % 2 == 1:
            pairs.append((dev(x, z, c), dev((x + step) % 4, z, c)))
        else:
            pairs.append((dev(x, z, c), dev(x, (z + step) % 4, c)))
    return pairs


def hop(value, axis, step):
    return lax.ppermute(value, "expert", along(axis, step % 4))


def swap(value):
    return lax.ppermute(value, "expert", SWAP)


def hop_dp(value, step):
    return lax.ppermute(value, "dp", [(y, (y + step) % 4) for y in range(4)])


def call(body, outs, ins, flops=0, moved=1 << 20, scratch=(), smem=0, anywhere=0, outs_anywhere=(), limit=48):
    flat = [outs] if not isinstance(outs, list) else outs
    specs = [HBM if i in outs_anywhere else VMEM for i in range(len(flat))]
    return pl.pallas_call(
        body,
        out_shape=outs,
        in_specs=[SMEM] * smem + [VMEM] * (len(ins) - smem - anywhere) + [HBM] * anywhere,
        out_specs=specs if isinstance(outs, list) else specs[0],
        scratch_shapes=list(scratch),
        compiler_params=pltpu.CompilerParams(vmem_limit_bytes=limit * 1024 * 1024),
        cost_estimate=pl.CostEstimate(flops=flops, bytes_accessed=moved, transcendentals=0),
    )(*ins)


def shape(dims, dtype):
    return jax.ShapeDtypeStruct(dims, dtype)


def tie(*values):
    return lax.optimization_barrier(values)


def mm(a, b):
    return lax.dot_general(a, b, (((1,), (0,)), ((), ())), preferred_element_type=F32)


def mm_nt(a, b):
    return lax.dot_general(a, b, (((1,), (1,)), ((), ())), preferred_element_type=F32)


def mm_tn(a, b):
    return lax.dot_general(a, b, (((0,), (0,)), ((), ())), preferred_element_type=F32)


def started(copies):
    for copy in copies:
        copy.start()
    return copies


def routing_body(eid_ref, own0, own1, own2, own3, v_ref, named_ref, sems):
    loads = started(
        [
            pltpu.make_async_copy(own.at[GTOK : GTOK + 16 * GRP], named_ref.at[g], sems.at[g])
            for g, own in enumerate((own0, own1, own2, own3))
        ]
    )
    eid = eid_ref[:, :]
    marks = []
    for g in range(GROUPS):
        loads[g].wait()
        for j in range(GRP):
            named = named_ref[g, 16 * j : 16 * j + 16, :].astype(F32)
            mark = jnp.zeros((NE, 256), F32)
            for k in range(16):
                mark = jnp.where(named[k : k + 1, :] == eid, 1.0, mark)
            marks.append(mark)
    before = lax.broadcasted_iota(jnp.int32, (TOK, TOK), 0) < lax.broadcasted_iota(jnp.int32, (TOK, TOK), 1)
    before = jnp.where(before, 1.0, 0.0).astype(BF)
    for p in range(2):
        stacked = jnp.concatenate([m[:, p * TOK : (p + 1) * TOK] for m in marks], axis=0)
        rank = mm(stacked.astype(BF), before)
        for g in range(GROUPS):
            for j in range(GRP):
                at = (g * GRP + j) * NE
                v_ref[p, g, :, j * TOK : (j + 1) * TOK] = jnp.where(
                    stacked[at : at + NE] > 0, rank[at : at + NE] + float(CAP * (j % 4)), -1.0
                )


def put_body(v_ref, put_ref):
    at_lane = lax.broadcasted_iota(jnp.int32, (TOK, QSLOT), 1)
    at_row = lax.broadcasted_iota(jnp.int32, (TOK, QSLOT), 0)
    spread = jnp.where((at_lane >= at_row * QCAP) & (at_lane < (at_row + 1) * QCAP), 1.0, 0.0).astype(BF)
    slot = lax.rem(lax.broadcasted_iota(jnp.int32, (1, QSLOT), 1), QCAP).astype(F32)
    for q in range(QUADS):
        v = v_ref[q // 2, :, (q % 2) * QTOK : (q % 2 + 1) * QTOK]
        turned = jnp.concatenate([v, jnp.zeros((TOK - NE, QTOK), F32)], axis=0).T.astype(BF)
        put_ref[q] = jnp.where(mm(turned, spread) == slot, 1.0, 0.0).astype(BF)


def gather_rows(v_ref, own, oth, near_ref, far_ref, x_ref, sems):
    near = [pltpu.make_async_copy(own[g].at[0:GTOK], near_ref.at[g], sems.at[g]) for g in range(GROUPS)]
    far = [
        [
            pltpu.make_async_copy(
                oth[d].at[g * 256 : (g + 1) * 256], far_ref.at[g, d * 256 : (d + 1) * 256], sems.at[4 + 4 * g + d]
            )
            for d in range(4)
        ]
        for g in range(GROUPS)
    ]
    for g in range(GROUPS):
        near[g].start()
        started(far[g])
    slot = lax.broadcasted_iota(jnp.int32, (QCAP, QTOK), 0).astype(F32)
    for g in range(GROUPS):
        near[g].wait()
        for copy in far[g]:
            copy.wait()
        rows = []
        for i in range(2):
            span = slice(i * QTOK, (i + 1) * QTOK)
            v = v_ref[g, :, span]
            pick = jnp.concatenate([jnp.where(slot == v[e : e + 1, :], 1.0, 0.0) for e in range(NE)], axis=0).astype(BF)
            rows.append((mm(pick, near_ref[g, span, :]), mm(pick, far_ref[g, span, :])))
        for e in range(NE):
            at = slice(e * QCAP, (e + 1) * QCAP)
            for h in range(2):
                x_ref[e, g * GSLOT : (g + 1) * GSLOT, h * HALF : (h + 1) * HALF] = jnp.concatenate(
                    [rows[0][h][at], rows[1][h][at]], axis=0
                ).astype(BF)


def halves(sc_ref):
    core = sc_ref[1]
    return (
        pl.ds(pl.multiple_of(core * HALF, HALF), HALF),
        pl.ds(pl.multiple_of((1 - core) * HALF, HALF), HALF),
    )


def expert_at(sc_ref, e):
    return lax.rem(2 * sc_ref[0] + e, NE)


def up_body(sc_ref, v_ref, sel_ref, w_hbm, *refs):
    own, oth, x_hbm, parts = refs[0:4], refs[4:8], refs[8], refs[9:13]
    near_ref, far_ref, x_ref, w_up_ref, sems, w_sem, x_sem = refs[13:]
    load = pltpu.make_async_copy(w_hbm, w_up_ref, w_sem)
    load.start()
    gather_rows(v_ref, own, oth, near_ref, far_ref, x_ref, sems)
    store = pltpu.make_async_copy(x_ref, x_hbm, x_sem)
    store.start()
    load.wait()
    first, second = halves(sc_ref)
    sel = sel_ref[:, :]
    lane_pad = jnp.zeros((1, 192), F32)
    for dy in range(4):
        heads, tails = [], []
        for i in range(2):
            e = 2 * dy + i
            at = expert_at(sc_ref, e)
            rows = x_ref[e]
            total = mm(rows[:, :HALF], w_up_ref[at, first, :]) + mm(rows[:, HALF:], w_up_ref[at, second, :])
            parts[dy][i * ESLOT : (i + 1) * ESLOT, :] = total.astype(BF)
            logit = mm_nt(sel, rows)[e : e + 1, :]
            heads.append(logit[:, :256])
            tails.append(jnp.concatenate([logit[:, 256:], lane_pad], axis=1))
        logits = jnp.concatenate(heads + tails, axis=0)
        high = logits.astype(BF).astype(F32)
        low = logits - high
        parts[dy][OWN:, :] = jnp.concatenate([high, low, jnp.zeros((8, 256), F32)], axis=0).astype(BF)
    store.wait()


def down_grad_body(sc_ref, v_ref, w_hbm, *refs):
    own, oth, x_hbm, parts = refs[0:4], refs[4:8], refs[8], refs[9:13]
    near_ref, far_ref, x_ref, w_down_ref, sems, w_sem, x_sem = refs[13:]
    load = pltpu.make_async_copy(w_hbm, w_down_ref, w_sem)
    load.start()
    gather_rows(v_ref, own, oth, near_ref, far_ref, x_ref, sems)
    store = pltpu.make_async_copy(x_ref, x_hbm, x_sem)
    store.start()
    load.wait()
    first, second = halves(sc_ref)
    for e in range(NE):
        at = expert_at(sc_ref, e)
        rows = x_ref[e]
        total = mm_nt(rows[:, :HALF], w_down_ref[at, :, first]) + mm_nt(rows[:, HALF:], w_down_ref[at, :, second])
        parts[e // 2][(e % 2) * ESLOT : (e % 2 + 1) * ESLOT, :] = total.astype(BF)
    store.wait()


def as_columns(rows):
    turned = jnp.concatenate([rows, jnp.zeros((TOK - rows.shape[0], 256), F32)], axis=0).T
    return jnp.concatenate([turned[:, 0:1], turned[:64, 2:3], turned[:, 1:2], turned[:64, 3:4]], axis=0)


def as_rows(column):
    wide = jnp.broadcast_to(column, (OWN, TOK))
    lane = lax.broadcasted_iota(jnp.int32, (256, TOK), 1)
    pad = jnp.zeros((192, TOK), F32)
    pieces = (
        wide[0:256],
        wide[ESLOT : ESLOT + 256],
        jnp.concatenate([wide[256:ESLOT], pad], axis=0),
        jnp.concatenate([wide[ESLOT + 256 :], pad], axis=0),
    )
    mixed = jnp.zeros((256, TOK), F32)
    for i, piece in enumerate(pieces):
        mixed = jnp.where(lane == i, piece, mixed)
    return mixed.T[:EXT]


def settle_body(p0, p1, p2, p3, hid_ref, pre_ref, gate_ref):
    def total(lo, hi):
        return sum(p[lo:hi, :].astype(F32) for p in (p0, p1, p2, p3))

    extra = total(OWN, OWN + EXT)
    gate = jax.nn.sigmoid(as_columns(extra[0:4] + extra[4:8]))
    pre = total(0, OWN)
    pre_ref[:, :] = pre
    gate_ref[:, :] = jnp.broadcast_to(gate, (OWN, TOK))
    inner = GELU_C * (pre + GELU_A * pre * pre * pre)
    hid_ref[:, :] = (gate * (0.5 * pre * (1.0 + jnp.tanh(inner)))).astype(BF)


def settle_grad_body(p0, p1, p2, p3, pre_ref, gate_ref, grad_ref):
    total = sum(p[:, :].astype(F32) for p in (p0, p1, p2, p3))
    pre = pre_ref[:, :]
    gate = gate_ref[:, 0:1]
    tangent = jnp.tanh(GELU_C * (pre + GELU_A * pre * pre * pre))
    hidden = (0.5 * pre * (1.0 + tangent)).astype(BF).astype(F32)
    slope = 0.5 * (1.0 + tangent) + 0.5 * pre * (1.0 - tangent * tangent) * GELU_C * (1.0 + 3.0 * GELU_A * pre * pre)
    score = jnp.sum(hidden * total, axis=1, keepdims=True)
    grad_ref[0:OWN, :] = (gate * total * slope).astype(BF)
    grad_ref[OWN:, :] = as_rows(score * gate * (1.0 - gate)).astype(BF)


def place_rows(out_ref, e, pair):
    for q in range(QUADS):
        span = slice(q * QCAP, (q + 1) * QCAP)
        out_ref[q, e * QCAP : (e + 2) * QCAP, :] = jnp.concatenate([pair[0][span], pair[1][span]], axis=0).astype(BF)


def scatter_rows(put_hbm, put_ref, loads, out_ref, y_hbm, y_ref, y_sems, far):
    stores = []
    for q in range(QUADS):
        loads[q].wait()
        rows = mm(put_ref[q], out_ref[q]).astype(BF)
        g, i = q // 2, q % 2
        for k in range(2):
            d = 2 * i + k
            at = ((d * 4 + g) if far else (g * 4 + d)) * 256
            y_ref[at : at + 256, :] = rows[k * 256 : (k + 1) * 256]
            stores.append(pltpu.make_async_copy(y_ref.at[at : at + 256], y_hbm.at[at : at + 256], y_sems.at[2 * q + k]))
            stores[-1].start()
    for copy in stores:
        copy.wait()


def load_all(sc_ref, w_view, w_ref, w_sem, hid_hbm, hid_ref, hid_sems, put_hbm, put_ref, put_sems):
    w_load = pltpu.make_async_copy(w_view, w_ref, w_sem)
    hid_loads = [pltpu.make_async_copy(hid_hbm[d], hid_ref.at[d], hid_sems.at[d]) for d in range(4)]
    put_loads = [pltpu.make_async_copy(put_hbm.at[q], put_ref.at[q], put_sems.at[q]) for q in range(QUADS)]
    hid_loads[0].start()
    w_load.start()
    started(hid_loads[1:])
    started(put_loads)
    w_load.wait()
    return hid_loads, put_loads


def down_body(far, sc_ref, put_hbm, w_hbm, h0, h1, h2, h3, y_hbm, y_ref, out_ref, w_ref, hid_ref, put_ref, w_sem, hid_sems, put_sems, y_sems):
    cols = halves(sc_ref)[1 if far else 0]
    hid_loads, put_loads = load_all(
        sc_ref, w_hbm.at[:, :, cols], w_ref, w_sem, (h0, h1, h2, h3), hid_ref, hid_sems, put_hbm, put_ref, put_sems
    )
    for d in range(4):
        hid_loads[d].wait()
        pair = [
            mm(hid_ref[d, i * ESLOT : (i + 1) * ESLOT, :], w_ref[expert_at(sc_ref, 2 * d + i)]) for i in range(2)
        ]
        place_rows(out_ref, 2 * d, pair)
    scatter_rows(put_hbm, put_ref, put_loads, out_ref, y_hbm, y_ref, y_sems, far)


def logit_rows(extras):
    rows = []
    for extra in extras:
        extra = extra.astype(F32)
        for i in range(2):
            rows.append(jnp.concatenate([extra[i : i + 1, :], extra[2 + i : 3 + i, :64]], axis=1))
    return jnp.concatenate(rows, axis=0)


def up_grad_body(far, sc_ref, sel_ref, put_hbm, w_hbm, h0, h1, h2, h3, y_hbm, y_ref, out_ref, w_ref, hid_ref, put_ref, w_sem, hid_sems, put_sems, y_sems):
    part = slice(HALF, 2 * HALF) if far else slice(0, HALF)
    rows = halves(sc_ref)[1 if far else 0]
    hid_loads, put_loads = load_all(
        sc_ref, w_hbm.at[:, rows, :], w_ref, w_sem, (h0, h1, h2, h3), hid_ref, hid_sems, put_hbm, put_ref, put_sems
    )
    sel = sel_ref[:, part].astype(F32)
    for copy in hid_loads:
        copy.wait()
    rows = logit_rows([hid_ref[d, OWN:, :] for d in range(4)])
    rows = jnp.concatenate([rows, jnp.zeros((NE, 64), F32)], axis=1)
    columns = jnp.concatenate([rows, jnp.zeros((TOK - NE, 384), F32)], axis=0).T
    for d in range(4):
        pair = []
        for i in range(2):
            e = 2 * d + i
            out = mm_nt(hid_ref[d, i * ESLOT : (i + 1) * ESLOT, :], w_ref[expert_at(sc_ref, e)])
            pair.append(out + columns[:ESLOT, e : e + 1] * sel[e : e + 1, :])
        place_rows(out_ref, 2 * d, pair)
    scatter_rows(put_hbm, put_ref, put_loads, out_ref, y_hbm, y_ref, y_sems, far)


def d_down_body(sc_ref, c0_ref, c1_ref, *refs):
    hid, d_ref = (refs[0:4], refs[4:8]), refs[8]
    first, second = halves(sc_ref)
    for e in range(NE):
        at = expert_at(sc_ref, e)
        span = slice((e % 2) * ESLOT, (e % 2 + 1) * ESLOT)
        for h, cols in enumerate((first, second)):
            part = slice(h * HALF, (h + 1) * HALF)
            d_ref[at, :, cols] = mm_tn(hid[0][e // 2][span, :], c0_ref[e, :, part]) + mm_tn(
                hid[1][e // 2][span, :], c1_ref[e, :, part]
            )


def d_up_body(sc_ref, x0_ref, x1_ref, *refs):
    grads, d_ref = (refs[0:4], refs[4:8]), refs[8]
    first, second = halves(sc_ref)
    for e in range(NE):
        at = expert_at(sc_ref, e)
        span = slice((e % 2) * ESLOT, (e % 2 + 1) * ESLOT)
        for h, cols in enumerate((first, second)):
            part = slice(h * HALF, (h + 1) * HALF)
            d_ref[at, cols, :] = mm_tn(x0_ref[e, :, part], grads[0][e // 2][span, :]) + mm_tn(
                x1_ref[e, :, part], grads[1][e // 2][span, :]
            )


def d_sel_body(sc_ref, x0_ref, x1_ref, *refs):
    grads, sel_ref = (refs[0:4], refs[4:8]), refs[8]
    first, second = halves(sc_ref)
    rows = [logit_rows([g[OWN:, :] for g in grads[p]]).astype(BF) for p in range(2)]
    for e in range(NE):
        at = expert_at(sc_ref, e)
        d_sel = (mm(rows[0], x0_ref[e]) + mm(rows[1], x1_ref[e]))[e : e + 1, :]
        sel_ref[pl.ds(at, 1), first] = d_sel[:, :HALF]
        sel_ref[pl.ds(at, 1), second] = d_sel[:, HALF:]


def d_sel_order_body(place_ref, own_ref, oth_ref, out_ref, all_ref):
    place = place_ref[0]
    x, z, core = place // 8, lax.rem(place // 2, 4), lax.rem(place, 2)
    for source, side in ((own_ref, core), (oth_ref, 1 - core)):
        for second in range(4):
            for first in range(4):
                dx = jnp.where(side == 0, first, second)
                dz = jnp.where(side == 0, second, first)
                to = ((lax.rem(x + dx, 4) * 4 + lax.rem(z + dz, 4)) * 2 + side) * NE
                at = (second * 4 + first) * NE
                all_ref[pl.ds(pl.multiple_of(to, NE), NE), :] = source[at : at + NE, :]
    out_ref[:, :] = all_ref[:, :].T


def add_swapped_body(own_hbm, got_hbm, o0, o1, o2, o3, own_ref, got_ref, out_ref, sems):
    outs = (o0, o1, o2, o3)
    order = (2, 1, 3, 0)
    loads = {}
    for g in order:
        span = slice(g * GTOK, (g + 1) * GTOK)
        loads[g] = started(
            [
                pltpu.make_async_copy(own_hbm.at[span], own_ref.at[g], sems.at[3 * g]),
                pltpu.make_async_copy(got_hbm.at[span], got_ref.at[g], sems.at[3 * g + 1]),
            ]
        )
    stores = []
    for g in order:
        for copy in loads[g]:
            copy.wait()
        out_ref[g] = (own_ref[g].astype(F32) + got_ref[g].astype(F32)).astype(BF)
        stores.append(pltpu.make_async_copy(out_ref.at[g], outs[g], sems.at[3 * g + 2]))
        stores[-1].start()
    for copy in stores:
        copy.wait()


def add_second_body(a, b, c, d, *outs):
    for i in range(4):
        span = slice(i * 256, (i + 1) * 256)
        outs[i][:, :] = sum(r[span, :].astype(F32) for r in (a, b, c, d)).astype(BF)


def no_work(values):
    return values


def gather_chip(mine, beside=no_work, values=()):
    pieces = [mine] + [hop(mine, 1, -d) for d in (1, 2, 3)]
    rows = 2 * TOK
    stacked = jnp.concatenate([q[:rows] for q in pieces] + [q[rows:] for q in pieces if q.shape[0] > rows], axis=0)
    if beside is not no_work:
        stacked, values = tie(stacked, values)
    own = [stacked] + [hop(stacked, 2, -d) for d in (2, 1, 3)]
    own = [own[0], own[2], own[1], own[3]]
    oth = [swap(q) for q in own]
    if beside is not no_work:
        oth, values = tie(oth, beside(values))
        return own, oth, values
    return own, oth


def scatter_chip(own, oth, beside=no_work, values=()):
    outs = [shape((GTOK, HALF), BF)] * 4
    block = (GROUPS, GTOK, HALF)
    second = call(
        add_swapped_body,
        outs,
        (own, swap(oth)),
        moved=6 << 20,
        scratch=[pltpu.VMEM(block, BF)] * 3 + [pltpu.SemaphoreType.DMA((12,))],
        anywhere=2,
        outs_anywhere=(0, 1, 2, 3),
    )
    if beside is not no_work:
        second, values = tie(second, values)
    sent = {d: hop(second[d], 2, d) for d in (2, 1, 3)}
    got = [second[0], sent[1], sent[2], sent[3]]
    if beside is not no_work:
        got, values = tie(got, beside(values))
    first = call(add_second_body, [shape((2 * TOK, HALF), BF)] * 4, got, moved=3 << 20)
    sent = {d: hop(first[d], 1, d) for d in (2, 1, 3)}
    terms = [first[0], sent[1], sent[2], sent[3]]
    if beside is not no_work:
        return terms, values
    return terms


def all_dp(block):
    sent = {d: hop_dp(block, -d) for d in (2, 1, 3)}
    return [block, sent[1], sent[2], sent[3]]


def to_dp(parts):
    sent = {d: hop_dp(parts[d], d) for d in (2, 1, 3)}
    return [parts[0], sent[1], sent[2], sent[3]]


def per_device(tokens, picks, halting, w_sel, w_up, w_down, cotangent):
    dp = lax.axis_index("dp")
    place = lax.axis_index("expert")
    core = lax.rem(place, 2)
    sc = jnp.stack([dp, core]).astype(jnp.int32)
    rel = lax.rem(2 * dp + jnp.arange(NE, dtype=jnp.int32), NE) + NE * place
    eid = jnp.broadcast_to(rel.astype(F32)[:, None], (NE, 256))
    sel = w_sel.T[rel]
    sel = jnp.where(core == 0, sel, jnp.concatenate([sel[:, HALF:], sel[:, :HALF]], axis=1))

    def mine_of(array):
        return jnp.where(core == 0, array[:, :HALF], array[:, HALF:])

    def rest_of(array):
        return jnp.where(core == 0, array[:, HALF:], array[:, :HALF])

    def by_core(mine, rest):
        return jnp.where(core == 0, jnp.concatenate([mine, rest], axis=0), jnp.concatenate([rest, mine], axis=0))

    live = halting[None, :, None] > jnp.arange(2, dtype=jnp.int32)[:, None, None]
    named = jnp.where(live, picks, 256).transpose(2, 0, 1).reshape(16, 256).astype(BF)
    rest = swap(jnp.concatenate([rest_of(tokens), named], axis=0))
    state = by_core(mine_of(tokens), rest[:TOK])
    cot = by_core(mine_of(cotangent), swap(rest_of(cotangent)))

    own, oth = gather_chip(jnp.concatenate([state, by_core(named, rest[TOK:])], axis=0))
    v = call(
        routing_body,
        shape((2, GROUPS, NE, GTOK), F32),
        (eid, *own),
        moved=1 << 20,
        scratch=[pltpu.VMEM((GROUPS, 16 * GRP, 256), BF), pltpu.SemaphoreType.DMA((GROUPS,))],
        anywhere=4,
    )

    rows_type = shape((NE, ESLOT, 2 * HALF), BF)
    gather_flops = 2 * 640 * 1024 * 512 * 4 + 2 * 2560 * 512 * 256

    def gather_scratch(w):
        return [
            pltpu.VMEM((GROUPS, GTOK, HALF), BF),
            pltpu.VMEM((GROUPS, GTOK, HALF), BF),
            pltpu.VMEM((NE, ESLOT, 2 * HALF), BF),
            pltpu.VMEM(w.shape, BF),
            pltpu.SemaphoreType.DMA((20,)),
            pltpu.SemaphoreType.DMA,
            pltpu.SemaphoreType.DMA,
        ]

    def project_up(v, own, oth):
        return call(
            up_body,
            [rows_type] + [shape((OWN + EXT, HID), BF)] * 4,
            (sc, v, sel, w_up, *own, *oth),
            flops=gather_flops,
            moved=12 << 20,
            scratch=gather_scratch(w_up),
            smem=1,
            anywhere=9,
            outs_anywhere=(0,),
        )

    def project_cot(v, own, oth):
        return call(
            down_grad_body,
            [rows_type] + [shape((OWN, HID), BF)] * 4,
            (sc, v, w_down, *own, *oth),
            flops=gather_flops,
            moved=12 << 20,
            scratch=gather_scratch(w_down),
            smem=1,
            anywhere=9,
            outs_anywhere=(0,),
        )

    def settle(parts):
        outs = [shape((OWN, HID), BF), shape((OWN, HID), F32), shape((OWN, TOK), F32)]
        return call(settle_body, outs, parts, moved=3 << 20)

    def settle_grad(parts, pre, gate):
        return call(settle_grad_body, shape((OWN + EXT, HID), BF), (*parts, pre, gate), moved=3 << 20)

    def put_of(v):
        return call(put_body, shape((QUADS, QTOK, QSLOT), BF), (v,), flops=4096 * 384 * 256, moved=4 << 20)

    def spread_scratch(w_block, hid_rows):
        return [
            pltpu.VMEM((GROUPS * GTOK, HALF), BF),
            pltpu.VMEM((QUADS, QSLOT, HALF), BF),
            pltpu.VMEM((NE,) + w_block, BF),
            pltpu.VMEM((4, hid_rows, HID), BF),
            pltpu.VMEM((QUADS, QTOK, QSLOT), BF),
            pltpu.SemaphoreType.DMA,
            pltpu.SemaphoreType.DMA((4,)),
            pltpu.SemaphoreType.DMA((QUADS,)),
            pltpu.SemaphoreType.DMA((2 * QUADS,)),
        ]

    y_type = shape((GROUPS * GTOK, HALF), BF)

    def outputs(put, hid, far):
        return call(
            functools.partial(down_body, far),
            y_type,
            (sc, put, w_down, *hid),
            flops=gather_flops // 2,
            moved=8 << 20,
            scratch=spread_scratch((HID, HALF), OWN),
            smem=1,
            anywhere=6,
            outs_anywhere=(0,),
        )

    def grads_in(put, grads, far):
        return call(
            functools.partial(up_grad_body, far),
            y_type,
            (sc, sel, put, w_up, *grads),
            flops=gather_flops // 2,
            moved=8 << 20,
            scratch=spread_scratch((HALF, HID), OWN + EXT),
            smem=1,
            anywhere=6,
            outs_anywhere=(0,),
        )

    def advance(base, terms):
        return (base.astype(F32) + sum(t.astype(F32) for t in terms)).astype(BF)

    x0, *parts = project_up(v[0], own, oth)
    cot, parts = tie(cot, parts)
    cot_own, cot_oth = gather_chip(cot)
    hid0, pre0, gate0 = settle(to_dp(parts))
    put0, put1 = put_of(v[0]), put_of(v[1])
    hid0 = all_dp(hid0)
    c1, *cot_parts = project_cot(v[1], cot_own, cot_oth)
    hid0, cot_parts, put0, put1 = tie(hid0, cot_parts, put0, put1)
    far0 = outputs(put0, hid0, True)
    far0, near_hid = tie(far0, hid0)
    cot_parts = to_dp(cot_parts)
    state1 = advance(state, scatter_chip(outputs(put0, near_hid, False), far0))

    own, oth = gather_chip(state1)
    x1, *parts = project_up(v[1], own, oth)
    hid1, pre1, gate1 = settle(to_dp(parts))
    grad1 = all_dp(settle_grad(cot_parts, pre1, gate1))

    hid1, grad1 = tie(hid1, grad1)
    far1 = grads_in(put1, grad1, True)
    hid1 = all_dp(hid1)
    far1, near_grad1 = tie(far1, grad1)
    cot1 = advance(cot, scatter_chip(grads_in(put1, near_grad1, False), far1))

    def forward_outputs(values):
        put, hid = values
        return outputs(put, hid, True), outputs(put, hid, False)

    cot_own, cot_oth, (out_far, out_near) = gather_chip(cot1, forward_outputs, (put1, hid1))

    c0, *cot_parts = project_cot(v[0], cot_own, cot_oth)
    out_far, out_near, cot_parts = tie(out_far, out_near, cot_parts)
    cot_parts = to_dp(cot_parts)
    state2 = advance(state1, scatter_chip(out_near, out_far))
    grad0 = settle_grad(cot_parts, pre0, gate0)
    c0, grad0 = tie(c0, grad0)
    d_down = call(
        d_down_body,
        shape(w_down.shape, F32),
        (sc, c0, c1, *hid0, *hid1),
        flops=4 * 2560 * 512 * 256,
        moved=16 << 20,
        smem=1,
    )
    grad0 = all_dp(grad0)
    grad0, d_down, state2 = tie(grad0, d_down, state2)
    far0 = grads_in(put0, grad0, True)
    far0, near_grad0 = tie(far0, grad0)
    near0 = grads_in(put0, near_grad0, False)

    def last_work(values):
        grads = values
        d_sel = call(
            d_sel_body, shape((NE, 2 * HALF), F32), (sc, x0, x1, *grads, *grad1), moved=8 << 20, smem=1
        )
        first = jnp.concatenate([d_sel] + [hop(d_sel, 1, -d) for d in (1, 2, 3)], axis=0)
        d_up = call(
            d_up_body,
            shape(w_up.shape, F32),
            (sc, x0, x1, *grads, *grad1),
            flops=4 * 2560 * 512 * 256,
            moved=16 << 20,
            smem=1,
        )
        return first, d_up

    terms, (d_sel, d_up) = scatter_chip(near0, far0, last_work, grad0)
    d_sel = jnp.concatenate([d_sel] + [hop(d_sel, 2, -d) for d in (1, 2, 3)], axis=0)
    d_sel = call(
        d_sel_order_body,
        shape((2 * HALF, EXPERTS), F32),
        (place.reshape(1).astype(jnp.int32), d_sel, swap(d_sel)),
        scratch=[pltpu.VMEM((EXPERTS, 2 * HALF), F32)],
        smem=1,
    )
    cot0 = advance(cot1, terms)

    def whole(array):
        mine = jnp.where(core == 0, array[:TOK], array[TOK:])
        rest = swap(jnp.where(core == 0, array[TOK:], array[:TOK]))
        return jnp.where(
            core == 0, jnp.concatenate([mine, rest], axis=1), jnp.concatenate([rest, mine], axis=1)
        )

    return (whole(state2), whole(cot0), d_up, d_down, d_sel)


def solution(mesh):
    in_specs = (
        P("expert", "dp"),
        P(None, "expert", None),
        P("expert"),
        P("dp", None),
        P("expert", "dp", None),
        P("expert", None, "dp"),
        P("expert", "dp"),
    )
    out_specs = (
        P("expert", "dp"),
        P("expert", "dp"),
        P("expert", "dp", None),
        P("expert", None, "dp"),
        P("dp", None),
    )
    return jax.shard_map(
        per_device, mesh=mesh, in_specs=in_specs, out_specs=out_specs, check_vma=False
    )
```

time: 520 us -> 466 us (0.90)
  waiting for transfers between devices: 191 us -> 142 us
  starting transfers between devices: 131 us -> 170 us
  blocking collectives: 24.9 us -> 0 us
  local copies, waits for them, and re-layouts: 27 us -> 13.9 us
    all_gather x1 -> x0, blocking collectives: 24.9 us -> none  [per_device(): d_sel = lax.all_gather(d_sel, 'expert', axis=0, tiled=True).T]
    ppermute x48 -> x54, starting transfers between devices: 46.8 us -> 71.6 us  [hop(): return lax.ppermute(value, 'expert', along(axis, step % 4))]
    ppermute x48 -> x54, waiting for transfers between devices: 96.2 us -> 73.4 us  [hop(): return lax.ppermute(value, 'expert', along(axis, step % 4))]
    ppermute x24, waiting for transfers between devices: 84 us -> 61.3 us  [hop_dp(): return lax.ppermute(value, 'dp', [(y, (y + step) % 4) for y in range(4)])]
    ppermute x24, starting transfers between devices: 25.7 us -> 39.3 us  [hop_dp(): return lax.ppermute(value, 'dp', [(y, (y + step) % 4) for y in range(4)])]
    unnamed x170 -> x101, local copies, waits for them, and re-layouts: 22.4 us -> 13.2 us
    pallas_call x23 -> x31, Pallas kernels: 129 us -> 125 us  [call(): pl.pallas_call(body, out_shape=outs, in_specs=[SMEM] * smem + [VMEM] * (l...]
    ppermute x24 -> x25, waiting for transfers between devices: 10.8 us -> 7.58 us  [swap(): return lax.ppermute(value, 'expert', SWAP)]
  transfers between devices with their start and end apart: 96 -> 103, of which waited for: 46 -> 52; matrix products, arithmetic and copies ran while one was open for 2% -> 1% of each run, Pallas kernels for 16% -> 15%
where the time goes in v2:
time: 466 us; the launch traced here: 458 us
  starting transfers between devices  170 us (36%)
  waiting for transfers between devices  142 us (30%)
  Pallas kernels  125 us (27%)
  local copies, waits for them, and re-layouts  13.9 us (3%)
    pallas_call x31, Pallas kernels, call(): pl.pallas_call(body, out_shape=outs, in_specs=[SMEM] * smem + [VMEM] * (l...  125 us
    ppermute x54, waiting for transfers between devices, hop(): return lax.ppermute(value, 'expert', along(axis, step % 4))  73.4 us
    ppermute x54, starting transfers between devices, hop(): return lax.ppermute(value, 'expert', along(axis, step % 4))  71.6 us
    ppermute x24, waiting for transfers between devices, hop_dp(): return lax.ppermute(value, 'dp', [(y, (y + step) % 4) for y in range(4)])  61.3 us
    ppermute x25, starting transfers between devices, swap(): return lax.ppermute(value, 'expert', SWAP)  59 us
    ppermute x24, starting transfers between devices, hop_dp(): return lax.ppermute(value, 'dp', [(y, (y + step) % 4) for y in range(4)])  39.3 us
    unnamed x101, local copies, waits for them, and re-layouts  13.2 us
  transfers between devices with their start and end apart: 103, of which 52 were waited for; matrix products, arithmetic and copies ran while one was open for 1% of the time, Pallas kernels for 15%

profile of v2, /device:TPU:1, one launch (start us, length us, event | category | flops | bytes accessed | tf_op | source)
XLA Modules:
  0.0 457.7 jit_solution(7711312397832002011)
XLA Ops:
  5.5 3.9 collective-permute-start.1
  11.5 3.7 collective-permute-done.2
  28.7 5.1 %collective-permute-done.5.own2.refs_2_ = bf16[1152,256]{1,0:T(8,128)(2,1)S(1)} collective-permute-done((bf16[1152,256]{1,0:T(8,128)(2,1)S(1)}, bf16[1152,256]{1,0:T(8,128)(2,1)S(1)}, u32[]{:S(2)}, u32[]{:S(2)}) %collective-permute-start.5) | collective-permute-done | bytes 589856 | tf_op jit(solution)/shard_map/ppermute | solution.py:56
  39.0 7.2 %shard_map.111 = (bf16[8,320,512]{2,1,0:T(8,128)(2,1)}, bf16[656,256]{1,0:T(8,128)(2,1)S(1)}, bf16[656,256]{1,0:T(8,128)(2,1)S(1)}, bf16[656,256]{1,0:T(8,128)(2,1)S(1)}, bf16[656,256]{1,0:T(8,128)(2,1)S(1)}) custom-call(s32[2]{0:T(128)S(1)} %pad_add_fusion.sc_ref, f32[4,8,1024]{2,1,0:T(8,128)S(1)} %get-tuple-element.274.v_ref, ...), custom_call_target="tpu_custom_call" | custom-call | flops 3355443200 | bytes 12582912 | tf_op jit(solution)/shard_map/pallas_call | solution.py:70
  50.4 3.0 collective-permute-done.19
  60.7 3.7 collective-permute-done.12.p1
  64.3 8.2 %collective-permute-start.24 = (bf16[1024,256]{1,0:T(8,128)(2,1)S(1)}, bf16[1024,256]{1,0:T(8,128)(2,1)S(1)}, u32[]{:S(2)}, u32[]{:S(2)}) collective-permute-start(bf16[1024,256]{1,0:T(8,128)(2,1)S(1)} %constant_dynamic-update-slice_fusion.5.refs_0_), channel_id=1, source_target_pairs={{0,1},{1,0},{2,3},{3,2},{4,5},{5,4},{6,7},{7,6},{8,9},{9,8},{10,11... | collective-permute-start | bytes 1572872 | tf_op jit(solution)/shard_map/ppermute | solution.py:60
  73.2 3.2 collective-permute-start.14
  79.1 4.0 collective-permute-done.14.p3
  92.7 7.2 %shard_map.113 = (bf16[8,320,512]{2,1,0:T(8,128)(2,1)}, bf16[640,256]{1,0:T(8,128)(2,1)S(1)}, bf16[640,256]{1,0:T(8,128)(2,1)S(1)}, bf16[640,256]{1,0:T(8,128)(2,1)S(1)}, bf16[640,256]{1,0:T(8,128)(2,1)S(1)}) custom-call(s32[2]{0:T(128)S(1)} %pad_add_fusion.sc_ref, f32[4,8,1024]{2,1,0:T(8,128)S(1)} %get-tuple-element.273.v_ref, bf16[8,256,512]{2,1,0:T(8,128)(2,1)} %w_hbm.21, ...), custom_call_target="tpu_custom_call" | custom-call | flops 3355443200 | bytes 12582912 | tf_op jit(solution)/shard_map/pallas_call | solution.py:70
  101.9 8.4 %shard_map.116 = bf16[4096,256]{1,0:T(8,128)(2,1)S(1)} custom-call(s32[2]{0:T(128)S(1)} %pad_add_fusion.sc_ref, bf16[8,512,320]{2,1,0:T(8,128)(2,1)} %copy-done, bf16[8,256,512]{2,1,0:T(8,128)(2,1)S(1)} %copy-done.2, bf16[640,256]{1,0:T(8,128)(2,1)S(1)} %get-tuple-element.158.h0.refs_0_, bf16[640,256]{1,0:T(8,128)(2,1)S(1)} %collective-permute-done.15.h1.refs_1_, ...), custom_call_target="tpu_custom_call" | custom-call | flops 1677721600 | bytes 8388608 | tf_op jit(solution)/shard_map/pallas_call | solution.py:70
  112.5 8.4 %shard_map.117.own_hbm = bf16[4096,256]{1,0:T(8,128)(2,1)S(1)} custom-call(s32[2]{0:T(128)S(1)} %pad_add_fusion.sc_ref, bf16[8,512,320]{2,1,0:T(8,128)(2,1)} %copy-done, bf16[8,256,512]{2,1,0:T(8,128)(2,1)S(1)} %copy-done.2, bf16[640,256]{1,0:T(8,128)(2,1)S(1)} %get-tuple-element.158.h0.refs_0_, bf16[640,256]{1,0:T(8,128)(2,1)S(1)} %collective-permute-done.15.h1.refs_1_, ...), custom_call_target="tpu_custom_call" | custom-call | flops 1677721600 | bytes 8388608 | tf_op jit(solution)/shard_map/pallas_call | solution.py:70
  127.0 5.4 %collective-permute-done.29.b = bf16[1024,256]{1,0:T(8,128)(2,1)S(1)} collective-permute-done((bf16[1024,256]{1,0:T(8,128)(2,1)S(1)}, bf16[1024,256]{1,0:T(8,128)(2,1)S(1)}, u32[]{:S(2)}, u32[]{:S(2)}) %collective-permute-start.29) | collective-permute-done | bytes 524320 | tf_op jit(solution)/shard_map/ppermute | solution.py:56
  132.4 6.6 %collective-permute-done.30.c = bf16[1024,256]{1,0:T(8,128)(2,1)S(1)} collective-permute-done((bf16[1024,256]{1,0:T(8,128)(2,1)S(1)}, bf16[1024,256]{1,0:T(8,128)(2,1)S(1)}, u32[]{:S(2)}, u32[]{:S(2)}) %collective-permute-start.30) | collective-permute-done | bytes 524320 | tf_op jit(solution)/shard_map/ppermute | solution.py:56
  158.3 4.6 %collective-permute-start.41 = (bf16[1024,256]{1,0:T(8,128)(2,1)S(1)}, bf16[1024,256]{1,0:T(8,128)(2,1)S(1)}, u32[]{:S(2)}, u32[]{:S(2)}) collective-permute-start(bf16[1024,256]{1,0:T(8,128)(2,1)S(1)} %pad_maximum_fusion.refs_0_), channel_id=1, source_target_pairs={{0,1},{1,0},{2,3},{3,2},{4,5},{5,4},{6,7},{7,6},{8,9},{9,8},{10,11... | collective-permute-start | bytes 1572872 | tf_op jit(solution)/shard_map/ppermute | solution.py:60
  164.4 4.6 collective-permute-start.44
  170.6 4.4 collective-permute-start.43
  177.3 7.1 %shard_map.120 = (bf16[8,320,512]{2,1,0:T(8,128)(2,1)}, bf16[656,256]{1,0:T(8,128)(2,1)S(1)}, bf16[656,256]{1,0:T(8,128)(2,1)S(1)}, bf16[656,256]{1,0:T(8,128)(2,1)S(1)}, bf16[656,256]{1,0:T(8,128)(2,1)S(1)}) custom-call(s32[2]{0:T(128)S(1)} %pad_add_fusion.sc_ref, f32[4,8,1024]{2,1,0:T(8,128)S(1)} %get-tuple-element.273.v_ref, ...), custom_call_target="tpu_custom_call" | custom-call | flops 3355443200 | bytes 12582912 | tf_op jit(solution)/shard_map/pallas_call | solution.py:70
  190.9 3.9 collective-permute-done.45.p1
  195.6 7.0 %collective-permute-done.46.p2 = bf16[656,256]{1,0:T(8,128)(2,1)S(1)} collective-permute-done((bf16[656,256]{1,0:T(8,128)(2,1)S(1)}, bf16[656,256]{1,0:T(8,128)(2,1)S(1)}, u32[]{:S(2)}, u32[]{:S(2)}) %collective-permute-start.46) | collective-permute-done | bytes 335904 | tf_op jit(solution)/shard_map/ppermute | solution.py:64
  203.3 5.7 %collective-permute-done.48.p1 = bf16[640,256]{1,0:T(8,128)(2,1)S(1)} collective-permute-done((bf16[640,256]{1,0:T(8,128)(2,1)S(1)}, bf16[640,256]{1,0:T(8,128)(2,1)S(1)}, u32[]{:S(2)}, u32[]{:S(2)}) %collective-permute-start.48) | collective-permute-done | bytes 327712 | tf_op jit(solution)/shard_map/ppermute | solution.py:64
  209.0 7.6 %collective-permute-done.49.p2 = bf16[640,256]{1,0:T(8,128)(2,1)S(1)} collective-permute-done((bf16[640,256]{1,0:T(8,128)(2,1)S(1)}, bf16[640,256]{1,0:T(8,128)(2,1)S(1)}, u32[]{:S(2)}, u32[]{:S(2)}) %collective-permute-start.49) | collective-permute-done | bytes 327712 | tf_op jit(solution)/shard_map/ppermute | solution.py:64
  218.6 3.1 collective-permute-start.52
  222.6 4.9 %collective-permute-done.53.h3.refs_7_ = bf16[656,256]{1,0:T(8,128)(2,1)S(1)} collective-permute-done((bf16[656,256]{1,0:T(8,128)(2,1)S(1)}, bf16[656,256]{1,0:T(8,128)(2,1)S(1)}, u32[]{:S(2)}, u32[]{:S(2)}) %collective-permute-start.53) | collective-permute-done | bytes 335904 | tf_op jit(solution)/shard_map/ppermute | solution.py:64
  227.5 8.8 %collective-permute-done.52.h2.refs_6_ = bf16[656,256]{1,0:T(8,128)(2,1)S(1)} collective-permute-done((bf16[656,256]{1,0:T(8,128)(2,1)S(1)}, bf16[656,256]{1,0:T(8,128)(2,1)S(1)}, u32[]{:S(2)}, u32[]{:S(2)}) %collective-permute-start.52) | collective-permute-done | bytes 335904 | tf_op jit(solution)/shard_map/ppermute | solution.py:64
  236.3 8.4 %shard_map.123 = bf16[4096,256]{1,0:T(8,128)(2,1)S(1)} custom-call(s32[2]{0:T(128)S(1)} %pad_add_fusion.sc_ref, bf16[8,512]{1,0:T(8,128)(2,1)S(1)} %maximum_select_fusion.5.sel_ref, bf16[8,512,320]{2,1,0:T(8,128)(2,1)} %copy-done.1, bf16[8,512,256]{2,1,0:T(8,128)(2,1)S(1)} %copy-done.3, bf16[656,256]{1,0:T(8,128)(2,1)S(1)} %shard_map.122.h0.refs_4_, ...), custom_call_target="tpu_custom_call" | custom-call | flops 1677721600 | bytes 8388608 | tf_op jit(solution)/shard_map/pallas_call | solution.py:70
  246.6 8.4 %shard_map.124.own_hbm = bf16[4096,256]{1,0:T(8,128)(2,1)S(1)} custom-call(s32[2]{0:T(128)S(1)} %pad_add_fusion.sc_ref, bf16[8,512]{1,0:T(8,128)(2,1)S(1)} %maximum_select_fusion.5.sel_ref, bf16[8,512,320]{2,1,0:T(8,128)(2,1)} %copy-done.1, bf16[8,512,256]{2,1,0:T(8,128)(2,1)S(1)} %copy-done.3, bf16[656,256]{1,0:T(8,128)(2,1)S(1)} %shard_map.122.h0.refs_4_, ...), custom_call_target="tpu_custom_call" | custom-call | flops 1677721600 | bytes 8388608 | tf_op jit(solution)/shard_map/pallas_call | solution.py:70
  258.9 2.9 collective-permute-start.56
  261.8 6.0 %collective-permute-done.55.b = bf16[1024,256]{1,0:T(8,128)(2,1)S(1)} collective-permute-done((bf16[1024,256]{1,0:T(8,128)(2,1)S(1)}, bf16[1024,256]{1,0:T(8,128)(2,1)S(1)}, u32[]{:S(2)}, u32[]{:S(2)}) %collective-permute-start.55) | collective-permute-done | bytes 524320 | tf_op jit(solution)/shard_map/ppermute | solution.py:56
  267.8 6.5 %collective-permute-done.56.c = bf16[1024,256]{1,0:T(8,128)(2,1)S(1)} collective-permute-done((bf16[1024,256]{1,0:T(8,128)(2,1)S(1)}, bf16[1024,256]{1,0:T(8,128)(2,1)S(1)}, u32[]{:S(2)}, u32[]{:S(2)}) %collective-permute-start.56) | collective-permute-done | bytes 524320 | tf_op jit(solution)/shard_map/ppermute | solution.py:56
  286.4 3.2 collective-permute-start.62
  293.8 4.3 collective-permute-done.65.h2.refs_6_
  302.7 4.6 %collective-permute-start.70 = (bf16[1024,256]{1,0:T(8,128)(2,1)S(1)}, bf16[1024,256]{1,0:T(8,128)(2,1)S(1)}, u32[]{:S(2)}, u32[]{:S(2)}) collective-permute-start(bf16[1024,256]{1,0:T(8,128)(2,1)S(1)} %pad_maximum_fusion.1.refs_0_), channel_id=1, source_target_pairs={{0,1},{1,0},{2,3},{3,2},{4,5},{5,4},{6,7},{7,6},{8,9},{9,8},{10,11... | collective-permute-start | bytes 1572872 | tf_op jit(solution)/shard_map/ppermute | solution.py:60
  309.2 2.9 collective-permute-start.73
  312.1 3.1 collective-permute-done.68.refs_2_
  315.1 2.9 collective-permute-start.72
  318.7 8.4 %shard_map.128.own_hbm = bf16[4096,256]{1,0:T(8,128)(2,1)S(1)} custom-call(s32[2]{0:T(128)S(1)} %pad_add_fusion.sc_ref, bf16[8,512,320]{2,1,0:T(8,128)(2,1)} %copy-done.1, bf16[8,256,512]{2,1,0:T(8,128)(2,1)S(1)} %copy-done.2, bf16[640,256]{1,0:T(8,128)(2,1)S(1)} %get-tuple-element.202.h0.refs_4_, bf16[640,256]{1,0:T(8,128)(2,1)S(1)} %collective-permute-done.64.h1.refs_5_, ...), custom_call_target="tpu_custom_call" | custom-call | flops 1677721600 | bytes 8388608 | tf_op jit(solution)/shard_map/pallas_call | solution.py:70
  327.2 8.4 %shard_map.127 = bf16[4096,256]{1,0:T(8,128)(2,1)S(1)} custom-call(s32[2]{0:T(128)S(1)} %pad_add_fusion.sc_ref, bf16[8,512,320]{2,1,0:T(8,128)(2,1)} %copy-done.1, bf16[8,256,512]{2,1,0:T(8,128)(2,1)S(1)} %copy-done.2, bf16[640,256]{1,0:T(8,128)(2,1)S(1)} %get-tuple-element.202.h0.refs_4_, bf16[640,256]{1,0:T(8,128)(2,1)S(1)} %collective-permute-done.64.h1.refs_5_, ...), custom_call_target="tpu_custom_call" | custom-call | flops 1677721600 | bytes 8388608 | tf_op jit(solution)/shard_map/pallas_call | solution.py:70
  343.1 5.9 %shard_map.129 = (bf16[8,320,512]{2,1,0:T(8,128)(2,1)}, bf16[640,256]{1,0:T(8,128)(2,1)S(1)}, bf16[640,256]{1,0:T(8,128)(2,1)S(1)}, bf16[640,256]{1,0:T(8,128)(2,1)S(1)}, bf16[640,256]{1,0:T(8,128)(2,1)S(1)}) custom-call(s32[2]{0:T(128)S(1)} %pad_add_fusion.sc_ref, f32[4,8,1024]{2,1,0:T(8,128)S(1)} %copy-done.13, bf16[8,256,512]{2,1,0:T(8,128)(2,1)} %w_hbm.21, ...), custom_call_target="tpu_custom_call" | custom-call | flops 3355443200 | bytes 12582912 | tf_op jit(solution)/shard_map/pallas_call | solution.py:70
  349.8 3.6 collective-permute-done.80.got_hbm
  367.3 4.1 collective-permute-done.82.c
  381.8 6.2 %shard_map.131 = f32[8,256,512]{2,1,0:T(8,128)} custom-call(s32[2]{0:T(128)S(1)} %pad_add_fusion.sc_ref, bf16[8,320,512]{2,1,0:T(8,128)(2,1)S(1)} %copy-done.7, bf16[8,320,512]{2,1,0:T(8,128)(2,1)} %get-tuple-element.225.c1_ref, bf16[640,256]{1,0:T(8,128)(2,1)S(1)} %get-tuple-element.158.h0.refs_0_, bf16[640,256]{1,0:T(8,128)(2,1)S(1)} %collective-permute-done.15.h1.refs_1_, ...), custom_call_target="tpu_custom_call" | custom-call | flops 1342177280 | bytes 16777216 | tf_op jit(solution)/shard_map/pallas_call | solution.py:70
  388.1 7.6 %collective-permute-done.78.h2.refs_2_ = bf16[656,256]{1,0:T(8,128)(2,1)S(1)} collective-permute-done((bf16[656,256]{1,0:T(8,128)(2,1)S(1)}, bf16[656,256]{1,0:T(8,128)(2,1)S(1)}, u32[]{:S(2)}, u32[]{:S(2)}) %collective-permute-start.78) | collective-permute-done | bytes 335904 | tf_op jit(solution)/shard_map/ppermute | solution.py:64
  395.7 8.4 %shard_map.134 = bf16[4096,256]{1,0:T(8,128)(2,1)S(1)} custom-call(s32[2]{0:T(128)S(1)} %pad_add_fusion.sc_ref, bf16[8,512]{1,0:T(8,128)(2,1)S(1)} %maximum_select_fusion.5.sel_ref, bf16[8,512,320]{2,1,0:T(8,128)(2,1)} %copy-done, bf16[8,512,256]{2,1,0:T(8,128)(2,1)S(1)} %copy-done.3, bf16[656,256]{1,0:T(8,128)(2,1)S(1)} %shard_map.130.h0.refs_0_, ...), custom_call_target="tpu_custom_call" | custom-call | flops 1677721600 | bytes 8388608 | tf_op jit(solution)/shard_map/pallas_call | solution.py:70
  406.2 8.4 %shard_map.135.own_hbm = bf16[4096,256]{1,0:T(8,128)(2,1)S(1)} custom-call(s32[2]{0:T(128)S(1)} %pad_add_fusion.sc_ref, bf16[8,512]{1,0:T(8,128)(2,1)S(1)} %maximum_select_fusion.5.sel_ref, bf16[8,512,320]{2,1,0:T(8,128)(2,1)} %copy-done, bf16[8,512,256]{2,1,0:T(8,128)(2,1)S(1)} %copy-done.3, bf16[656,256]{1,0:T(8,128)(2,1)S(1)} %shard_map.130.h0.refs_0_, ...), custom_call_target="tpu_custom_call" | custom-call | flops 1677721600 | bytes 8388608 | tf_op jit(solution)/shard_map/pallas_call | solution.py:70
  428.7 6.3 %shard_map.138 = f32[8,512,256]{2,1,0:T(8,128)} custom-call(s32[2]{0:T(128)S(1)} %pad_add_fusion.sc_ref, bf16[8,320,512]{2,1,0:T(8,128)(2,1)S(1)} %copy-done.4, bf16[8,320,512]{2,1,0:T(8,128)(2,1)} %get-tuple-element.255.x1_ref, bf16[656,256]{1,0:T(8,128)(2,1)S(1)} %shard_map.130.h0.refs_0_, bf16[656,256]{1,0:T(8,128)(2,1)S(1)} %collective-permute-done.77.h1.refs_1_, ...), custom_call_target="tpu_custom_call" | custom-call | flops 1342177280 | bytes 16777216 | tf_op jit(solution)/shard_map/pallas_call | solution.py:70
  435.0 4.3 collective-permute-start.87
  448.7 3.2 collective-permute-start.102
  (324 shorter events, 188.3 us)
Async XLA Ops:
  17.5 16.3 %collective-permute-start.5 = (bf16[1152,256]{1,0:T(8,128)(2,1)S(1)}, bf16[1152,256]{1,0:T(8,128)(2,1)S(1)}, u32[]{:S(2)}, u32[]{:S(2)}) collective-permute-start(bf16[1152,256]{1,0:T(8,128)(2,1)S(1)} %constant_dynamic-update-slice_fusion.own0.refs_0_), channel_id=1, source_target_pairs={{0,4},{1,17},{2,6},{3,19},{4,0},{5,21},{6,2},{7,23},{8,12},{9,25},... | collective-permute-start | bytes 1769480 | tf_op jit(solution)/shard_map/ppermute | solution.py:56
  20.0 16.5 %collective-permute-start.4 = (bf16[1152,256]{1,0:T(8,128)(2,1)S(1)}, bf16[1152,256]{1,0:T(8,128)(2,1)S(1)}, u32[]{:S(2)}, u32[]{:S(2)}) collective-permute-start(bf16[1152,256]{1,0:T(8,128)(2,1)S(1)} %constant_dynamic-update-slice_fusion.own0.refs_0_), channel_id=1, source_target_pairs={{0,6},{1,25},{2,0},{3,27},{4,2},{5,29},{6,4},{7,31},{8,14},{9,1},{... | collective-permute-start | bytes 1769480 | tf_op jit(solution)/shard_map/ppermute | solution.py:56
  21.2 15.5 %collective-permute-start.7 = (bf16[128,256]{1,0:T(8,128)(2,1)S(1)}, bf16[128,256]{1,0:T(8,128)(2,1)S(1)}, u32[]{:S(2)}, u32[]{:S(2)}) collective-permute-start(bf16[128,256]{1,0:T(8,128)(2,1)S(1)} %get-tuple-element.280), channel_id=1, source_target_pairs={{0,1},{1,0},{2,3},{3,2},{4,5},{5,4},{6,7},{7,6},{8,9},{9,8},{10,11... | collective-permute-start | bytes 196616 | tf_op jit(solution)/shard_map/ppermute | solution.py:60
  24.2 13.5 %collective-permute-start.8 = (bf16[1152,256]{1,0:T(8,128)(2,1)S(1)}, bf16[1152,256]{1,0:T(8,128)(2,1)S(1)}, u32[]{:S(2)}, u32[]{:S(2)}) collective-permute-start(bf16[1152,256]{1,0:T(8,128)(2,1)S(1)} %constant_dynamic-update-slice_fusion.own0.refs_0_), channel_id=1, source_target_pairs={{0,1},{1,0},{2,3},{3,2},{4,5},{5,4},{6,7},{7,6},{8,9},{9,8},{10,11... | collective-permute-start | bytes 1769480 | tf_op jit(solution)/shard_map/ppermute | solution.py:60
  54.0 18.5 %collective-permute-start.23 = (bf16[1024,256]{1,0:T(8,128)(2,1)S(1)}, bf16[1024,256]{1,0:T(8,128)(2,1)S(1)}, u32[]{:S(2)}, u32[]{:S(2)}) collective-permute-start(bf16[1024,256]{1,0:T(8,128)(2,1)S(1)} %constant_dynamic-update-slice_fusion.5.refs_0_), channel_id=1, source_target_pairs={{0,2},{1,9},{2,4},{3,11},{4,6},{5,13},{6,0},{7,15},{8,10},{9,17},{... | collective-permute-start | bytes 1572872 | tf_op jit(solution)/shard_map/ppermute | solution.py:56
  54.1 18.4 %collective-permute-start.22 = (bf16[1024,256]{1,0:T(8,128)(2,1)S(1)}, bf16[1024,256]{1,0:T(8,128)(2,1)S(1)}, u32[]{:S(2)}, u32[]{:S(2)}) collective-permute-start(bf16[1024,256]{1,0:T(8,128)(2,1)S(1)} %constant_dynamic-update-slice_fusion.5.refs_0_), channel_id=1, source_target_pairs={{0,4},{1,17},{2,6},{3,19},{4,0},{5,21},{6,2},{7,23},{8,12},{9,25},... | collective-permute-start | bytes 1572872 | tf_op jit(solution)/shard_map/ppermute | solution.py:56
  56.7 16.4 %collective-permute-start.21 = (bf16[1024,256]{1,0:T(8,128)(2,1)S(1)}, bf16[1024,256]{1,0:T(8,128)(2,1)S(1)}, u32[]{:S(2)}, u32[]{:S(2)}) collective-permute-start(bf16[1024,256]{1,0:T(8,128)(2,1)S(1)} %constant_dynamic-update-slice_fusion.5.refs_0_), channel_id=1, source_target_pairs={{0,6},{1,25},{2,0},{3,27},{4,2},{5,29},{6,4},{7,31},{8,14},{9,1},{... | collective-permute-start | bytes 1572872 | tf_op jit(solution)/shard_map/ppermute | solution.py:56
  58.1 15.1 %collective-permute-start.13 = (bf16[656,256]{1,0:T(8,128)(2,1)S(1)}, bf16[656,256]{1,0:T(8,128)(2,1)S(1)}, u32[]{:S(2)}, u32[]{:S(2)}) collective-permute-start(bf16[656,256]{1,0:T(8,128)(2,1)S(1)} %get-tuple-element.145), channel_id=1, source_target_pairs={{0,64},{32,96},{64,0},{96,32},{1,65},{33,97},{65,1},{97,33},{2,66}... | collective-permute-start | bytes 1007624 | tf_op jit(solution)/shard_map/ppermute | solution.py:64
  64.3 22.1 %collective-permute-start.24 = (bf16[1024,256]{1,0:T(8,128)(2,1)S(1)}, bf16[1024,256]{1,0:T(8,128)(2,1)S(1)}, u32[]{:S(2)}, u32[]{:S(2)}) collective-permute-start(bf16[1024,256]{1,0:T(8,128)(2,1)S(1)} %constant_dynamic-update-slice_fusion.5.refs_0_), channel_id=1, source_target_pairs={{0,1},{1,0},{2,3},{3,2},{4,5},{5,4},{6,7},{7,6},{8,9},{9,8},{10,11... | collective-permute-start | bytes 1572872 | tf_op jit(solution)/shard_map/ppermute | solution.py:60
  72.5 15.7 %collective-permute-start.27 = (bf16[1024,256]{1,0:T(8,128)(2,1)S(1)}, bf16[1024,256]{1,0:T(8,128)(2,1)S(1)}, u32[]{:S(2)}, u32[]{:S(2)}) collective-permute-start(bf16[1024,256]{1,0:T(8,128)(2,1)S(1)} %collective-permute-done.23.refs_3_), channel_id=1, source_target_pairs={{0,1},{1,0},{2,3},{3,2},{4,5},{5,4},{6,7},{7,6},{8,9},{9,8},{10,11... | collective-permute-start | bytes 1572872 | tf_op jit(solution)/shard_map/ppermute | solution.py:60
  72.5 20.1 %collective-permute-start.26 = (bf16[1024,256]{1,0:T(8,128)(2,1)S(1)}, bf16[1024,256]{1,0:T(8,128)(2,1)S(1)}, u32[]{:S(2)}, u32[]{:S(2)}) collective-permute-start(bf16[1024,256]{1,0:T(8,128)(2,1)S(1)} %collective-permute-done.22.refs_2_), channel_id=1, source_target_pairs={{0,1},{1,0},{2,3},{3,2},{4,5},{5,4},{6,7},{7,6},{8,9},{9,8},{10,11... | collective-permute-start | bytes 1572872 | tf_op jit(solution)/shard_map/ppermute | solution.py:60
  73.1 19.6 %collective-permute-start.25 = (bf16[1024,256]{1,0:T(8,128)(2,1)S(1)}, bf16[1024,256]{1,0:T(8,128)(2,1)S(1)}, u32[]{:S(2)}, u32[]{:S(2)}) collective-permute-start(bf16[1024,256]{1,0:T(8,128)(2,1)S(1)} %collective-permute-done.21.refs_1_), channel_id=1, source_target_pairs={{0,1},{1,0},{2,3},{3,2},{4,5},{5,4},{6,7},{7,6},{8,9},{9,8},{10,11... | collective-permute-start | bytes 1572872 | tf_op jit(solution)/shard_map/ppermute | solution.py:60
  83.6 16.4 %collective-permute-start.17 = (bf16[640,256]{1,0:T(8,128)(2,1)S(1)}, bf16[640,256]{1,0:T(8,128)(2,1)S(1)}, u32[]{:S(2)}, u32[]{:S(2)}) collective-permute-start(bf16[640,256]{1,0:T(8,128)(2,1)S(1)} %get-tuple-element.158.h0.refs_0_), channel_id=1, source_target_pairs={{0,32},{32,64},{64,96},{96,0},{1,33},{33,65},{65,97},{97,1},{2,34}... | collective-permute-start | bytes 983048 | tf_op jit(solution)/shard_map/ppermute | solution.py:64
  86.4 15.2 %collective-permute-start.16 = (bf16[640,256]{1,0:T(8,128)(2,1)S(1)}, bf16[640,256]{1,0:T(8,128)(2,1)S(1)}, u32[]{:S(2)}, u32[]{:S(2)}) collective-permute-start(bf16[640,256]{1,0:T(8,128)(2,1)S(1)} %get-tuple-element.158.h0.refs_0_), channel_id=1, source_target_pairs={{0,64},{32,96},{64,0},{96,32},{1,65},{33,97},{65,1},{97,33},{2,66}... | collective-permute-start | bytes 983048 | tf_op jit(solution)/shard_map/ppermute | solution.py:64
  88.2 13.7 %collective-permute-start.15 = (bf16[640,256]{1,0:T(8,128)(2,1)S(1)}, bf16[640,256]{1,0:T(8,128)(2,1)S(1)}, u32[]{:S(2)}, u32[]{:S(2)}) collective-permute-start(bf16[640,256]{1,0:T(8,128)(2,1)S(1)} %get-tuple-element.158.h0.refs_0_), channel_id=1, source_target_pairs={{0,96},{32,0},{64,32},{96,64},{1,97},{33,1},{65,33},{97,65},{2,98}... | collective-permute-start | bytes 983048 | tf_op jit(solution)/shard_map/ppermute | solution.py:64
  123.9 15.1 %collective-permute-start.30 = (bf16[1024,256]{1,0:T(8,128)(2,1)S(1)}, bf16[1024,256]{1,0:T(8,128)(2,1)S(1)}, u32[]{:S(2)}, u32[]{:S(2)}) collective-permute-start(bf16[1024,256]{1,0:T(8,128)(2,1)S(1)} %get-tuple-element.165), channel_id=1, source_target_pairs={{0,4},{1,17},{2,6},{3,19},{4,0},{5,21},{6,2},{7,23},{8,12},{9,25},... | collective-permute-start | bytes 1572872 | tf_op jit(solution)/shard_map/ppermute | solution.py:56
  126.5 12.5 %collective-permute-start.31 = (bf16[1024,256]{1,0:T(8,128)(2,1)S(1)}, bf16[1024,256]{1,0:T(8,128)(2,1)S(1)}, u32[]{:S(2)}, u32[]{:S(2)}) collective-permute-start(bf16[1024,256]{1,0:T(8,128)(2,1)S(1)} %get-tuple-element.166), channel_id=1, source_target_pairs={{0,6},{1,25},{2,0},{3,27},{4,2},{5,29},{6,4},{7,31},{8,14},{9,1},{... | collective-permute-start | bytes 1572872 | tf_op jit(solution)/shard_map/ppermute | solution.py:56
  155.8 14.8 %collective-permute-start.39 = (bf16[1024,256]{1,0:T(8,128)(2,1)S(1)}, bf16[1024,256]{1,0:T(8,128)(2,1)S(1)}, u32[]{:S(2)}, u32[]{:S(2)}) collective-permute-start(bf16[1024,256]{1,0:T(8,128)(2,1)S(1)} %pad_maximum_fusion.refs_0_), channel_id=1, source_target_pairs={{0,4},{1,17},{2,6},{3,19},{4,0},{5,21},{6,2},{7,23},{8,12},{9,25},... | collective-permute-start | bytes 1572872 | tf_op jit(solution)/shard_map/ppermute | solution.py:56
  158.1 16.9 %collective-permute-start.38 = (bf16[1024,256]{1,0:T(8,128)(2,1)S(1)}, bf16[1024,256]{1,0:T(8,128)(2,1)S(1)}, u32[]{:S(2)}, u32[]{:S(2)}) collective-permute-start(bf16[1024,256]{1,0:T(8,128)(2,1)S(1)} %pad_maximum_fusion.refs_0_), channel_id=1, source_target_pairs={{0,6},{1,25},{2,0},{3,27},{4,2},{5,29},{6,4},{7,31},{8,14},{9,1},{... | collective-permute-start | bytes 1572872 | tf_op jit(solution)/shard_map/ppermute | solution.py:56
  158.3 17.4 %collective-permute-start.41 = (bf16[1024,256]{1,0:T(8,128)(2,1)S(1)}, bf16[1024,256]{1,0:T(8,128)(2,1)S(1)}, u32[]{:S(2)}, u32[]{:S(2)}) collective-permute-start(bf16[1024,256]{1,0:T(8,128)(2,1)S(1)} %pad_maximum_fusion.refs_0_), channel_id=1, source_target_pairs={{0,1},{1,0},{2,3},{3,2},{4,5},{5,4},{6,7},{7,6},{8,9},{9,8},{10,11... | collective-permute-start | bytes 1572872 | tf_op jit(solution)/shard_map/ppermute | solution.py:60
  185.6 17.0 %collective-permute-start.46 = (bf16[656,256]{1,0:T(8,128)(2,1)S(1)}, bf16[656,256]{1,0:T(8,128)(2,1)S(1)}, u32[]{:S(2)}, u32[]{:S(2)}) collective-permute-start(bf16[656,256]{1,0:T(8,128)(2,1)S(1)} %get-tuple-element.173), channel_id=1, source_target_pairs={{0,64},{32,96},{64,0},{96,32},{1,65},{33,97},{65,1},{97,33},{2,66}... | collective-permute-start | bytes 1007624 | tf_op jit(solution)/shard_map/ppermute | solution.py:64
  187.7 15.0 %collective-permute-start.47 = (bf16[656,256]{1,0:T(8,128)(2,1)S(1)}, bf16[656,256]{1,0:T(8,128)(2,1)S(1)}, u32[]{:S(2)}, u32[]{:S(2)}) collective-permute-start(bf16[656,256]{1,0:T(8,128)(2,1)S(1)} %get-tuple-element.174), channel_id=1, source_target_pairs={{0,96},{32,0},{64,32},{96,64},{1,97},{33,1},{65,33},{97,65},{2,98}... | collective-permute-start | bytes 1007624 | tf_op jit(solution)/shard_map/ppermute | solution.py:64
  189.7 19.3 %collective-permute-start.48 = (bf16[640,256]{1,0:T(8,128)(2,1)S(1)}, bf16[640,256]{1,0:T(8,128)(2,1)S(1)}, u32[]{:S(2)}, u32[]{:S(2)}) collective-permute-start(bf16[640,256]{1,0:T(8,128)(2,1)S(1)} %copy-done.27), channel_id=1, source_target_pairs={{0,32},{32,64},{64,96},{96,0},{1,33},{33,65},{65,97},{97,1},{2,34}... | collective-permute-start | bytes 983048 | tf_op jit(solution)/shard_map/ppermute | solution.py:64
  189.7 26.9 %collective-permute-start.49 = (bf16[640,256]{1,0:T(8,128)(2,1)S(1)}, bf16[640,256]{1,0:T(8,128)(2,1)S(1)}, u32[]{:S(2)}, u32[]{:S(2)}) collective-permute-start(bf16[640,256]{1,0:T(8,128)(2,1)S(1)} %get-tuple-element.178), channel_id=1, source_target_pairs={{0,64},{32,96},{64,0},{96,32},{1,65},{33,97},{65,1},{97,33},{2,66}... | collective-permute-start | bytes 983048 | tf_op jit(solution)/shard_map/ppermute | solution.py:64
  194.8 21.8 %collective-permute-start.50 = (bf16[640,256]{1,0:T(8,128)(2,1)S(1)}, bf16[640,256]{1,0:T(8,128)(2,1)S(1)}, u32[]{:S(2)}, u32[]{:S(2)}) collective-permute-start(bf16[640,256]{1,0:T(8,128)(2,1)S(1)} %get-tuple-element.179), channel_id=1, source_target_pairs={{0,96},{32,0},{64,32},{96,64},{1,97},{33,1},{65,33},{97,65},{2,98}... | collective-permute-start | bytes 983048 | tf_op jit(solution)/shard_map/ppermute | solution.py:64
  218.6 17.7 %collective-permute-start.52 = (bf16[656,256]{1,0:T(8,128)(2,1)S(1)}, bf16[656,256]{1,0:T(8,128)(2,1)S(1)}, u32[]{:S(2)}, u32[]{:S(2)}) collective-permute-start(bf16[656,256]{1,0:T(8,128)(2,1)S(1)} %shard_map.122.h0.refs_4_), channel_id=1, source_target_pairs={{0,64},{32,96},{64,0},{96,32},{1,65},{33,97},{65,1},{97,33},{2,66}... | collective-permute-start | bytes 1007624 | tf_op jit(solution)/shard_map/ppermute | solution.py:64
  221.7 14.6 %collective-permute-start.51 = (bf16[656,256]{1,0:T(8,128)(2,1)S(1)}, bf16[656,256]{1,0:T(8,128)(2,1)S(1)}, u32[]{:S(2)}, u32[]{:S(2)}) collective-permute-start(bf16[656,256]{1,0:T(8,128)(2,1)S(1)} %shard_map.122.h0.refs_4_), channel_id=1, source_target_pairs={{0,96},{32,0},{64,32},{96,64},{1,97},{33,1},{65,33},{97,65},{2,98}... | collective-permute-start | bytes 1007624 | tf_op jit(solution)/shard_map/ppermute | solution.py:64
  258.9 15.4 %collective-permute-start.56 = (bf16[1024,256]{1,0:T(8,128)(2,1)S(1)}, bf16[1024,256]{1,0:T(8,128)(2,1)S(1)}, u32[]{:S(2)}, u32[]{:S(2)}) collective-permute-start(bf16[1024,256]{1,0:T(8,128)(2,1)S(1)} %get-tuple-element.193), channel_id=1, source_target_pairs={{0,4},{1,17},{2,6},{3,19},{4,0},{5,21},{6,2},{7,23},{8,12},{9,25},... | collective-permute-start | bytes 1572872 | tf_op jit(solution)/shard_map/ppermute | solution.py:56
  283.6 14.5 %collective-permute-start.65 = (bf16[640,256]{1,0:T(8,128)(2,1)S(1)}, bf16[640,256]{1,0:T(8,128)(2,1)S(1)}, u32[]{:S(2)}, u32[]{:S(2)}) collective-permute-start(bf16[640,256]{1,0:T(8,128)(2,1)S(1)} %get-tuple-element.202.h0.refs_4_), channel_id=1, source_target_pairs={{0,64},{32,96},{64,0},{96,32},{1,65},{33,97},{65,1},{97,33},{2,66}... | collective-permute-start | bytes 983048 | tf_op jit(solution)/shard_map/ppermute | solution.py:64
  285.7 13.9 %collective-permute-start.64 = (bf16[640,256]{1,0:T(8,128)(2,1)S(1)}, bf16[640,256]{1,0:T(8,128)(2,1)S(1)}, u32[]{:S(2)}, u32[]{:S(2)}) collective-permute-start(bf16[640,256]{1,0:T(8,128)(2,1)S(1)} %get-tuple-element.202.h0.refs_4_), channel_id=1, source_target_pairs={{0,96},{32,0},{64,32},{96,64},{1,97},{33,1},{65,33},{97,65},{2,98}... | collective-permute-start | bytes 983048 | tf_op jit(solution)/shard_map/ppermute | solution.py:64
  300.3 14.8 %collective-permute-start.68 = (bf16[1024,256]{1,0:T(8,128)(2,1)S(1)}, bf16[1024,256]{1,0:T(8,128)(2,1)S(1)}, u32[]{:S(2)}, u32[]{:S(2)}) collective-permute-start(bf16[1024,256]{1,0:T(8,128)(2,1)S(1)} %pad_maximum_fusion.1.refs_0_), channel_id=1, source_target_pairs={{0,4},{1,17},{2,6},{3,19},{4,0},{5,21},{6,2},{7,23},{8,12},{9,25},... | collective-permute-start | bytes 1572872 | tf_op jit(solution)/shard_map/ppermute | solution.py:56
  302.7 15.4 %collective-permute-start.67 = (bf16[1024,256]{1,0:T(8,128)(2,1)S(1)}, bf16[1024,256]{1,0:T(8,128)(2,1)S(1)}, u32[]{:S(2)}, u32[]{:S(2)}) collective-permute-start(bf16[1024,256]{1,0:T(8,128)(2,1)S(1)} %pad_maximum_fusion.1.refs_0_), channel_id=1, source_target_pairs={{0,6},{1,25},{2,0},{3,27},{4,2},{5,29},{6,4},{7,31},{8,14},{9,1},{... | collective-permute-start | bytes 1572872 | tf_op jit(solution)/shard_map/ppermute | solution.py:56
  302.7 34.2 %collective-permute-start.70 = (bf16[1024,256]{1,0:T(8,128)(2,1)S(1)}, bf16[1024,256]{1,0:T(8,128)(2,1)S(1)}, u32[]{:S(2)}, u32[]{:S(2)}) collective-permute-start(bf16[1024,256]{1,0:T(8,128)(2,1)S(1)} %pad_maximum_fusion.1.refs_0_), channel_id=1, source_target_pairs={{0,1},{1,0},{2,3},{3,2},{4,5},{5,4},{6,7},{7,6},{8,9},{9,8},{10,11... | collective-permute-start | bytes 1572872 | tf_op jit(solution)/shard_map/ppermute | solution.py:60
  309.2 28.5 %collective-permute-start.73 = (bf16[1024,256]{1,0:T(8,128)(2,1)S(1)}, bf16[1024,256]{1,0:T(8,128)(2,1)}, u32[]{:S(2)}, u32[]{:S(2)}) collective-permute-start(bf16[1024,256]{1,0:T(8,128)(2,1)S(1)} %collective-permute-done.69.refs_3_), channel_id=1, source_target_pairs={{0,1},{1,0},{2,3},{3,2},{4,5},{5,4},{6,7},{7,6},{8,9},{9,8},{10,11... | collective-permute-start | bytes 1572872 | tf_op jit(solution)/shard_map/ppermute | solution.py:60
  315.1 22.5 %collective-permute-start.72 = (bf16[1024,256]{1,0:T(8,128)(2,1)S(1)}, bf16[1024,256]{1,0:T(8,128)(2,1)}, u32[]{:S(2)}, u32[]{:S(2)}) collective-permute-start(bf16[1024,256]{1,0:T(8,128)(2,1)S(1)} %collective-permute-done.68.refs_2_), channel_id=1, source_target_pairs={{0,1},{1,0},{2,3},{3,2},{4,5},{5,4},{6,7},{7,6},{8,9},{9,8},{10,11... | collective-permute-start | bytes 1572872 | tf_op jit(solution)/shard_map/ppermute | solution.py:60
  318.1 19.6 %collective-permute-start.71 = (bf16[1024,256]{1,0:T(8,128)(2,1)S(1)}, bf16[1024,256]{1,0:T(8,128)(2,1)}, u32[]{:S(2)}, u32[]{:S(2)}) collective-permute-start(bf16[1024,256]{1,0:T(8,128)(2,1)S(1)} %collective-permute-done.67.refs_1_), channel_id=1, source_target_pairs={{0,1},{1,0},{2,3},{3,2},{4,5},{5,4},{6,7},{7,6},{8,9},{9,8},{10,11... | collective-permute-start | bytes 1572872 | tf_op jit(solution)/shard_map/ppermute | solution.py:60
  356.1 15.3 %collective-permute-start.82 = (bf16[1024,256]{1,0:T(8,128)(2,1)S(1)}, bf16[1024,256]{1,0:T(8,128)(2,1)S(1)}, u32[]{:S(2)}, u32[]{:S(2)}) collective-permute-start(bf16[1024,256]{1,0:T(8,128)(2,1)S(1)} %get-tuple-element.230), channel_id=1, source_target_pairs={{0,4},{1,17},{2,6},{3,19},{4,0},{5,21},{6,2},{7,23},{8,12},{9,25},... | collective-permute-start | bytes 1572872 | tf_op jit(solution)/shard_map/ppermute | solution.py:56
  358.9 12.5 %collective-permute-start.83 = (bf16[1024,256]{1,0:T(8,128)(2,1)S(1)}, bf16[1024,256]{1,0:T(8,128)(2,1)S(1)}, u32[]{:S(2)}, u32[]{:S(2)}) collective-permute-start(bf16[1024,256]{1,0:T(8,128)(2,1)S(1)} %get-tuple-element.231), channel_id=1, source_target_pairs={{0,6},{1,25},{2,0},{3,27},{4,2},{5,29},{6,4},{7,31},{8,14},{9,1},{... | collective-permute-start | bytes 1572872 | tf_op jit(solution)/shard_map/ppermute | solution.py:56
  358.9 16.2 %collective-permute-start.74 = (bf16[640,256]{1,0:T(8,128)(2,1)S(1)}, bf16[640,256]{1,0:T(8,128)(2,1)S(1)}, u32[]{:S(2)}, u32[]{:S(2)}) collective-permute-start(bf16[640,256]{1,0:T(8,128)(2,1)S(1)} %copy-done.32), channel_id=1, source_target_pairs={{0,32},{32,64},{64,96},{96,0},{1,33},{33,65},{65,97},{97,1},{2,34}... | collective-permute-start | bytes 983048 | tf_op jit(solution)/shard_map/ppermute | solution.py:64
  359.9 17.1 %collective-permute-start.75 = (bf16[640,256]{1,0:T(8,128)(2,1)S(1)}, bf16[640,256]{1,0:T(8,128)(2,1)S(1)}, u32[]{:S(2)}, u32[]{:S(2)}) collective-permute-start(bf16[640,256]{1,0:T(8,128)(2,1)S(1)} %copy-done.30), channel_id=1, source_target_pairs={{0,64},{32,96},{64,0},{96,32},{1,65},{33,97},{65,1},{97,33},{2,66}... | collective-permute-start | bytes 983048 | tf_op jit(solution)/shard_map/ppermute | solution.py:64
  373.3 14.7 %collective-permute-start.85 = (bf16[256,256]{1,0:T(8,128)(2,1)S(1)}, bf16[256,256]{1,0:T(8,128)(2,1)S(1)}, u32[]{:S(2)}, u32[]{:S(2)}) collective-permute-start(bf16[256,256]{1,0:T(8,128)(2,1)S(1)} %get-tuple-element.234), channel_id=1, source_target_pairs={{0,16},{1,5},{2,18},{3,7},{4,20},{5,1},{6,22},{7,3},{8,24},{9,13},... | collective-permute-start | bytes 393224 | tf_op jit(solution)/shard_map/ppermute | solution.py:56
  375.1 12.9 %collective-permute-start.86 = (bf16[256,256]{1,0:T(8,128)(2,1)S(1)}, bf16[256,256]{1,0:T(8,128)(2,1)S(1)}, u32[]{:S(2)}, u32[]{:S(2)}) collective-permute-start(bf16[256,256]{1,0:T(8,128)(2,1)S(1)} %get-tuple-element.235), channel_id=1, source_target_pairs={{0,24},{1,7},{2,26},{3,1},{4,28},{5,3},{6,30},{7,5},{8,0},{9,15},{... | collective-permute-start | bytes 393224 | tf_op jit(solution)/shard_map/ppermute | solution.py:56
  379.0 16.7 %collective-permute-start.78 = (bf16[656,256]{1,0:T(8,128)(2,1)S(1)}, bf16[656,256]{1,0:T(8,128)(2,1)S(1)}, u32[]{:S(2)}, u32[]{:S(2)}) collective-permute-start(bf16[656,256]{1,0:T(8,128)(2,1)S(1)} %shard_map.130.h0.refs_0_), channel_id=1, source_target_pairs={{0,64},{32,96},{64,0},{96,32},{1,65},{33,97},{65,1},{97,33},{2,66}... | collective-permute-start | bytes 1007624 | tf_op jit(solution)/shard_map/ppermute | solution.py:64
  381.7 14.0 %collective-permute-start.77 = (bf16[656,256]{1,0:T(8,128)(2,1)S(1)}, bf16[656,256]{1,0:T(8,128)(2,1)S(1)}, u32[]{:S(2)}, u32[]{:S(2)}) collective-permute-start(bf16[656,256]{1,0:T(8,128)(2,1)S(1)} %shard_map.130.h0.refs_0_), channel_id=1, source_target_pairs={{0,96},{32,0},{64,32},{96,64},{1,97},{33,1},{65,33},{97,65},{2,98}... | collective-permute-start | bytes 1007624 | tf_op jit(solution)/shard_map/ppermute | solution.py:64
  416.6 22.7 %collective-permute-start.89 = (bf16[1024,256]{1,0:T(8,128)(2,1)S(1)}, bf16[1024,256]{1,0:T(8,128)(2,1)S(1)}, u32[]{:S(2)}, u32[]{:S(2)}) collective-permute-start(bf16[1024,256]{1,0:T(8,128)(2,1)S(1)} %get-tuple-element.251), channel_id=1, source_target_pairs={{0,2},{1,9},{2,4},{3,11},{4,6},{5,13},{6,0},{7,15},{8,10},{9,17},{... | collective-permute-start | bytes 1572872 | tf_op jit(solution)/shard_map/ppermute | solution.py:56
  417.6 21.7 %collective-permute-start.90 = (bf16[1024,256]{1,0:T(8,128)(2,1)S(1)}, bf16[1024,256]{1,0:T(8,128)(2,1)S(1)}, u32[]{:S(2)}, u32[]{:S(2)}) collective-permute-start(bf16[1024,256]{1,0:T(8,128)(2,1)S(1)} %get-tuple-element.252), channel_id=1, source_target_pairs={{0,4},{1,17},{2,6},{3,19},{4,0},{5,21},{6,2},{7,23},{8,12},{9,25},... | collective-permute-start | bytes 1572872 | tf_op jit(solution)/shard_map/ppermute | solution.py:56
  419.6 19.7 %collective-permute-start.91 = (bf16[1024,256]{1,0:T(8,128)(2,1)S(1)}, bf16[1024,256]{1,0:T(8,128)(2,1)S(1)}, u32[]{:S(2)}, u32[]{:S(2)}) collective-permute-start(bf16[1024,256]{1,0:T(8,128)(2,1)S(1)} %get-tuple-element.253), channel_id=1, source_target_pairs={{0,6},{1,25},{2,0},{3,27},{4,2},{5,29},{6,4},{7,31},{8,14},{9,1},{... | collective-permute-start | bytes 1572872 | tf_op jit(solution)/shard_map/ppermute | solution.py:56
  435.0 19.4 %collective-permute-start.87 = (bf16[128,256]{1,0:T(8,128)(2,1)S(1)}, bf16[128,256]{1,0:T(8,128)(2,1)S(1)}, u32[]{:S(2)}, u32[]{:S(2)}) collective-permute-start(bf16[128,256]{1,0:T(8,128)(2,1)S(1)} %get-tuple-element.278), channel_id=1, source_target_pairs={{0,1},{1,0},{2,3},{3,2},{4,5},{5,4},{6,7},{7,6},{8,9},{9,8},{10,11... | collective-permute-start | bytes 196616 | tf_op jit(solution)/shard_map/ppermute | solution.py:60
  (99 other events, 1015.6 us)
